TPU v7x, 1024 devices: a whole 8x8x8 slice. The times are simulated.
1024 devices in a mesh: grid: 64 (over y_lo, z, core), band: 16 (over x, y_hi).
Axes of the slice: x: 8, y: 8 (y_hi: 2, y_lo: 4; y = y_hi * 4 + y_lo), z: 8, core: 2. Of those that a mesh axis runs over, the one named last changes fastest.
Arguments:
- orbitals: float32 [64, 256, 6400], P('band', 'grid'), may hold values from -6 to 6
- potential: float32 [256, 6400], P('grid'), may hold values from -6 to 6
- projectors: float32 [3, 2, 8, 256, 6400], P(None, None, None, 'grid'), may hold values from -0.18 to 0.18
- kb_energy: float32 [64, 2, 8], P('grid'), may hold values from 0.3 to 3
- proj_count: int32 [64, 2], P('grid'), may hold values from 0 to 8, as said below
Outputs:
- hpsi: float32 [64, 256, 6400], P('band', 'grid')
- correlation: float32 [64, 64], P('band')
- projected: float32 [64, 64], P('band')
Inputs may be any that keep to these rules, and one draw needn't show every extreme that they name: `proj_count`: in each domain the live atom slots come first, 1 of them or more; live slots have 1 to 8 active projectors; some domain has all 2 slots live and some atom has all 8 projectors.
All inputs are finite; a program needn't handle non-finite values.
Results may differ from a plain program's by a relative error of at most 0.00005.
Values sent between devices are 32-bit elements; how exact they have to be, the bound alone decides.
A program may use at most 64 MiB of HBM per device.

v0:
```python
import jax
import jax.numpy as jnp
from jax import lax
from jax.sharding import PartitionSpec as P

NY = 80


STENCIL = (-205.0 / 72.0, 8.0 / 5.0, -1.0 / 5.0, 8.0 / 315.0, -1.0 / 560.0)


def extended(block, sides, width):
    for axis, dim in sides:
        count = lax.axis_size(axis)
        forward = [(i, i + 1) for i in range(count - 1)]
        forward.append((count - 1, 0))
        backward = [(target, source) for source, target in forward]
        low = lax.ppermute(
            lax.slice_in_dim(block, block.shape[dim] - width, None, axis=dim), axis, forward
        )
        high = lax.ppermute(lax.slice_in_dim(block, 0, width, axis=dim), axis, backward)
        block = jnp.concatenate([low, block, high], axis=dim)
    return block


def laplace(orbital_field, padded, row_width):
    layers = orbital_field.shape[1]
    cell_count = orbital_field.shape[2]
    column = lax.broadcasted_iota(jnp.int32, (cell_count,), 0) % row_width
    far_pad = jnp.pad(orbital_field, ((0, 0), (0, 0), (4 * row_width, 4 * row_width)))
    near_pad = jnp.pad(orbital_field, ((0, 0), (0, 0), (4, 4)))
    result = 3.0 * STENCIL[0] * orbital_field
    for offset in range(1, 5):
        above_z = padded[:, 4 + offset : 4 + offset + layers]
        below_z = padded[:, 4 - offset : 4 - offset + layers]
        upper_x = far_pad[:, :, (4 + offset) * row_width : (4 + offset) * row_width + cell_count]
        lower_x = far_pad[:, :, (4 - offset) * row_width : (4 - offset) * row_width + cell_count]
        right_y = jnp.where(
            column + offset < row_width, near_pad[:, :, 4 + offset : 4 + offset + cell_count], 0.0
        )
        left_y = jnp.where(
            column >= offset, near_pad[:, :, 4 - offset : 4 - offset + cell_count], 0.0
        )
        result = result + STENCIL[offset] * (
            above_z + below_z + upper_x + lower_x + right_y + left_y
        )
    return result


def contract_rows(first_mat, second_mat):
    return lax.dot_general(
        first_mat,
        second_mat,
        (((1,), (1,)), ((), ())),
        precision=lax.Precision.HIGHEST,
        preferred_element_type=jnp.float32,
    )


def shards(orbitals, potential, projectors, kb_energy, proj_count):
    groups, layers, cell_count = orbitals.shape
    atom_slots = projectors.shape[1]
    proj_kinds = projectors.shape[2]
    width_ap = atom_slots * proj_kinds
    padded = extended(orbitals, (("grid", 1),), 4)
    kinetic = -0.5 * laplace(orbitals, padded, NY)
    local_term = potential[None] * orbitals
    flat_bands = orbitals.reshape(groups, layers * cell_count)
    proj_table = projectors.reshape(3 * width_ap, layers * cell_count)
    partial_value = contract_rows(proj_table, flat_bands).reshape(3, width_ap, groups)
    domains = lax.axis_size("grid")
    own_index = lax.axis_index("grid")
    spread = jnp.zeros((domains, width_ap, groups), jnp.float32)
    for position in range(3):
        target = (own_index - 1 + position + domains) % domains
        spread = lax.dynamic_update_slice(
            spread, partial_value[position][None], (target, jnp.int32(0), jnp.int32(0))
        )
    summed = lax.psum(spread, "grid")
    owner_total = lax.dynamic_index_in_dim(summed, own_index, 0, keepdims=False)
    active = (
        lax.broadcasted_iota(jnp.int32, (atom_slots, proj_kinds), 1) < proj_count[0][:, None]
    ).astype(jnp.float32)
    weight = (kb_energy[0] * active).reshape(width_ap)
    owned_coefs = owner_total * weight[:, None]
    beside_all = extended(owned_coefs[None], (("grid", 0),), 1)
    nonlocal_term = lax.dot_general(
        beside_all.reshape(3 * width_ap, groups),
        proj_table,
        (((0,), (0,)), ((), ())),
        precision=lax.Precision.HIGHEST,
        preferred_element_type=jnp.float32,
    )
    hpsi = kinetic + local_term + nonlocal_term.reshape(groups, layers, cell_count)
    hflat = hpsi.reshape(groups, layers * cell_count)
    all_bands = lax.all_gather(flat_bands, "band", axis=0, tiled=True)
    correlation = contract_rows(flat_bands, all_bands)
    projected = contract_rows(hflat, all_bands)
    correlation, projected = lax.psum((correlation, projected), "grid")
    volume = 1.0 / (layers * cell_count * lax.axis_size("grid"))
    return (hpsi, correlation * volume, projected * volume)


def solution(mesh):
    in_specs = (
        P("band", "grid", None),
        P("grid", None),
        P(None, None, None, "grid", None),
        P("grid", None, None),
        P("grid", None),
    )
    out_specs = (P("band", "grid", None), P("band", None), P("band", None))
    return jax.shard_map(shards, mesh=mesh, in_specs=in_specs, out_specs=out_specs, check_vma=False)
```

profile of v0, /device:TPU:1, one launch (start us, length us, event | category | flops | bytes accessed | tf_op | source)
XLA Modules:
  0.0 514.5 jit_solution(3416281437530467984)
XLA Ops:
  7.2 2.0 reshape.56
  9.4 5.6 %copy.47 = f32[6,8,4,6400]{3,1,2,0:T(8,128)} copy(f32[6,8,4,6400]{3,2,1,0:T(4,128)} %bitcast.36) | data formatting | bytes 9830400
  14.9 0.1 copy.48
  15.1 0.1 lt.91
  15.2 0.1 squeeze.5
  15.3 5.7 %fusion.34 = f32[48,4]{0,1:T(4,128)S(1)} fusion(f32[48,25600]{1,0:T(8,128)} %bitcast.34, f32[4,25600]{1,0:T(4,128)S(1)} %bitcast.38), kind=kOutput, calls=%fused_computation.66 | convolution fusion | flops 58982400 | bytes 5325568 | tf_op jit(solution)/shard_map/dot_general | solution.py:51
  21.0 0.1 fusion.33
  21.3 293.3 %psum.21 = f32[64,16,4]{1,0,2:T(8,128)S(1)} all-reduce(f32[64,16,4]{1,0,2:T(8,128)S(1)} %dynamic_update_slice.11), channel_id=1, replica_groups=mesh['grid'=64,'band'=16] {'grid'}, use_global_device_ids=true, to_apply=%region_0.1 | all-reduce | flops 4096 | bytes 32768 | tf_op jit(solution)/shard_map/psum | solution.py:79
  314.6 3.6 collective-permute-start.2
  318.2 6.5 %collective-permute-start.3 = (f32[1,16,4]{1,0,2:T(1,128)S(1)}, f32[1,16,4]{1,0,2:T(1,128)S(1)}, u32[]{:S(2)}, u32[]{:S(2)}) collective-permute-start(f32[1,16,4]{1,0,2:T(1,128)S(1)} %dynamic-slice_multiply_fusion), channel_id=1, source_target_pairs={{16,0},{32,16},{48,32},{64,48},{80,64},{96,80},{112,96},{128,112},... | collective-permute-start | bytes 776 | tf_op jit(solution)/shard_map/ppermute | solution.py:21
  324.6 0.1 copy.33
  324.8 1.9 collective-permute-start.1
  326.7 7.5 %collective-permute-start = (f32[4,4,6400]{2,0,1:T(4,128)S(1)}, f32[4,4,6400]{2,0,1:T(4,128)S(1)}, u32[]{:S(2)}, u32[]{:S(2)}) collective-permute-start(f32[4,4,6400]{2,0,1:T(4,128)S(1)} %copy.33), channel_id=1, source_target_pairs={{16,0},{32,16},{48,32},{64,48},{80,64},{96,80},{112,96},{128,112},... | collective-permute-start | bytes 1228808 | tf_op jit(solution)/shard_map/ppermute | solution.py:21
  334.4 0.1 reshape.59
  334.5 0.2 constant_dynamic-update-slice_fusion.1
  334.7 1.3 collective-permute-done
  336.0 7.7 %convolution_add_fusion = f32[4,4,6400]{2,0,1:T(4,128)S(1)} fusion(f32[48,4,1]{0,1,2:T(4,128)S(1)} %reshape.59, f32[4,4,6400]{2,0,1:T(4,128)S(1)} %copy.33, f32[4,8,6400]{2,0,1:T(4,128)S(1)} %get-tuple-element.15, f32[4,8,6400]{2,0,1:T(4,128)S(1)} %constant_dynamic-update-slice_fusion, f32[4,4,6400]{2,0,1:T(4,128)S(1)} %collective-permute-done, ...), kind=kOutput, calls=%fused_computation | convolution fusion | flops 63180800 | bytes 9165568 | tf_op jit(solution)/shard_map/dot_general | solution.py:87
  343.7 0.9 copy.45
  344.6 7.0 %reshape.57 = f32[64,25600]{1,0:T(8,128)} reshape(f32[16,4,25600]{2,1,0:T(4,128)} %all-gather.3.cloned.1.call-done) | data formatting | bytes 13107200
  351.6 7.4 %fusion.35 = f32[4,64]{1,0:T(4,128)S(1)} fusion(f32[4,25600]{1,0:T(4,128)S(1)} %bitcast.39, f32[64,25600]{1,0:T(8,128)} %reshape.57), kind=kOutput, calls=%fused_computation.67 | convolution fusion | flops 78643200 | bytes 6964224 | tf_op jit(solution)/shard_map/dot_general | solution.py:51
  358.9 5.2 %fusion.36 = f32[4,64]{1,0:T(4,128)S(1)} fusion(f32[4,25600]{1,0:T(4,128)S(1)} %bitcast.40, f32[64,25600]{1,0:T(8,128)S(1)} %copy-done), kind=kOutput, calls=%fused_computation.68 | convolution fusion | flops 78643200 | bytes 6964224 | tf_op jit(solution)/shard_map/dot_general | solution.py:51
  364.1 142.4 %all-reduce.2 = (f32[4,64]{1,0:T(4,128)S(1)}, f32[4,64]{1,0:T(4,128)S(1)}) all-reduce(f32[4,64]{1,0:T(4,128)S(1)} %fusion.35, f32[4,64]{1,0:T(4,128)S(1)} %fusion.36), channel_id=1, replica_groups=mesh['grid'=64,'band'=16] {'grid'}, use_global_device_ids=true, to_apply=%region_1.2 | all-reduce | flops 512 | bytes 4096 | tf_op jit(solution)/shard_map/psum | solution.py:99
  506.5 0.6 broadcast_multiply_fusion
  507.1 0.6 broadcast_multiply_fusion.1
  (30 shorter events, 0.5 us)
Async XLA Ops:
  7.2 337.4 %all-gather.3.cloned.1.call-start = ((), (), s32[]{:S(2)}) async-start(), calls=%async_computation | async-start | bytes 6963200 | tf_op jit(solution)/shard_map/all_gather | solution.py:96
  9.3 5.6 %copy-start.1 = (f32[4,4,6400]{2,1,0:T(4,128)S(1)}, f32[4,4,6400]{2,1,0:T(4,128)}, u32[]{:S(2)}) copy-start(f32[4,4,6400]{2,1,0:T(4,128)} %param.5) | copy-start | bytes 1228804
  9.3 5.7 %copy-start.4 = (s32[1,2]{1,0:T(1,128)S(1)}, s32[1,2]{1,0:T(1,128)}, u32[]{:S(2)}) copy-start(s32[1,2]{1,0:T(1,128)} %param.9) | copy-start | bytes 28
  9.3 5.9 %copy-start.3 = (f32[1,2,8]{2,1,0:T(2,128)S(1)}, f32[1,2,8]{2,1,0:T(2,128)}, u32[]{:S(2)}) copy-start(f32[1,2,8]{2,1,0:T(2,128)} %param.8) | copy-start | bytes 196
  15.0 321.0 %copy-start.2 = (f32[4,6400]{1,0:T(4,128)S(1)}, f32[4,6400]{1,0:T(4,128)}, u32[]{:S(2)}) copy-start(f32[4,6400]{1,0:T(4,128)} %param.6) | copy-start | bytes 307204
  314.6 19.8 %collective-permute-start.2 = (f32[1,16,4]{1,0,2:T(1,128)S(1)}, f32[1,16,4]{1,0,2:T(1,128)S(1)}, u32[]{:S(2)}, u32[]{:S(2)}) collective-permute-start(f32[1,16,4]{1,0,2:T(1,128)S(1)} %dynamic-slice_multiply_fusion), channel_id=1, source_target_pairs={{0,16},{16,32},{32,48},{48,64},{64,80},{80,96},{96,112},{112,128},... | collective-permute-start | bytes 776 | tf_op jit(solution)/shard_map/ppermute | solution.py:18
  318.2 16.2 %collective-permute-start.3 = (f32[1,16,4]{1,0,2:T(1,128)S(1)}, f32[1,16,4]{1,0,2:T(1,128)S(1)}, u32[]{:S(2)}, u32[]{:S(2)}) collective-permute-start(f32[1,16,4]{1,0,2:T(1,128)S(1)} %dynamic-slice_multiply_fusion), channel_id=1, source_target_pairs={{16,0},{32,16},{48,32},{64,48},{80,64},{96,80},{112,96},{128,112},... | collective-permute-start | bytes 776 | tf_op jit(solution)/shard_map/ppermute | solution.py:21
  324.8 9.7 %collective-permute-start.1 = (f32[4,4,6400]{2,0,1:T(4,128)S(1)}, f32[4,4,6400]{2,0,1:T(4,128)S(1)}, u32[]{:S(2)}, u32[]{:S(2)}) collective-permute-start(f32[4,4,6400]{2,0,1:T(4,128)S(1)} %copy.33), channel_id=1, source_target_pairs={{0,16},{16,32},{32,48},{48,64},{64,80},{80,96},{96,112},{112,128},... | collective-permute-start | bytes 1228808 | tf_op jit(solution)/shard_map/ppermute | solution.py:18
  326.7 9.3 %collective-permute-start = (f32[4,4,6400]{2,0,1:T(4,128)S(1)}, f32[4,4,6400]{2,0,1:T(4,128)S(1)}, u32[]{:S(2)}, u32[]{:S(2)}) collective-permute-start(f32[4,4,6400]{2,0,1:T(4,128)S(1)} %copy.33), channel_id=1, source_target_pairs={{16,0},{32,16},{48,32},{64,48},{80,64},{96,80},{112,96},{128,112},... | collective-permute-start | bytes 1228808 | tf_op jit(solution)/shard_map/ppermute | solution.py:21
  351.6 7.4 %copy-start = (f32[64,25600]{1,0:T(8,128)S(1)}, f32[64,25600]{1,0:T(8,128)}, u32[]{:S(2)}) copy-start(f32[64,25600]{1,0:T(8,128)} %reshape.57) | copy-start | bytes 19660804
Sparse Core Ops, SparseCore 0:
  12.3 183.4 all-gather.2
where the time goes:
time: 524 us; the launch traced here: 514 us
  blocking collectives  436 us (83%)
  matrix products  26 us (5%)
  starting transfers between devices  19.6 us (4%)
  local copies, waits for them, and re-layouts  16.4 us (3%)
  between operations  14.2 us (3%)
    psum x1, blocking collectives, shards(): summed = lax.psum(spread, 'grid')  293 us
    psum x1, blocking collectives, shards(): correlation, projected = lax.psum((correlation, projected), 'grid')  142 us
    dot_general x3, matrix products, contract_rows(): lax.dot_general(first_mat, second_mat, (((1,), (1,)), ((), ())), precisio...  18.3 us
    unnamed x18, local copies, waits for them, and re-layouts  15.9 us
    ppermute x2, starting transfers between devices, extended(): lax.ppermute(lax.slice_in_dim(block, 0, width, axis=dim), axis, backward)  14 us
  transfers between devices with their start and end apart: 5, of which 1 were waited for; matrix products, arithmetic and copies ran while one was open for 4% of the time, Pallas kernels for 0%

commit v1 on v0

v1 whole, which is shorter than its diff:
```python
import functools

import jax
import jax.numpy as jnp
from jax import lax
from jax.experimental import pallas as pl
from jax.experimental.pallas import tpu as pltpu
from jax.sharding import PartitionSpec as P

NY = 80
STENCIL = (-205.0 / 72.0, 8.0 / 5.0, -1.0 / 5.0, 8.0 / 315.0, -1.0 / 560.0)
MESH = pl.DeviceIdType.MESH
LANES = 128
PAD = 384
CHUNK = 640
WIDE = 1280


def iota(rows, cols):
    return (
        lax.broadcasted_iota(jnp.int32, (rows, cols), 0),
        lax.broadcasted_iota(jnp.int32, (rows, cols), 1),
    )


def ones_where(condition):
    return jnp.where(condition, 1.0, 0.0).astype(jnp.float32)


def dot(a, b, dims):
    return lax.dot_general(
        a,
        b,
        (dims, ((), ())),
        precision=lax.Precision.HIGHEST,
        preferred_element_type=jnp.float32,
    )


NN = ((1,), (0,))
NT = ((1,), (1,))
TN = ((0,), (0,))


def z_matrix():
    row, col = iota(16, 48)
    same = ((row >> 2) & 3) == ((col >> 2) & 3)
    diff = (col >> 4) * 4 + (col & 3) - 4 - (row & 3)
    dist = jnp.abs(diff)
    value = jnp.zeros((16, 48), jnp.float32)
    for k in range(1, 5):
        value = jnp.where(dist == k, -0.5 * STENCIL[k], value)
    return jnp.where(same, value, 0.0)


def kernel(
    dims,
    psi_in,
    pot_in,
    table_in,
    weight_in,
    h_out,
    corr_out,
    gram_out,
    psi,
    before,
    after,
    pot,
    table,
    h,
    got_psi,
    got_h,
    ycoef,
    part,
    low1,
    high1,
    low2,
    high2,
    terms,
    band_terms,
    own_sum,
    pair_terms,
    pair_sum,
    line_terms,
    in_sem,
    table_sem,
    halo_send,
    halo_recv,
    part_send,
    part_recv,
    psi_send,
    psi_recv,
    h_send,
    h_recv,
    extra_send,
    extra_recv,
    out_sem,
    a_send,
    a_recv,
    b_send,
    b_recv,
    c_send,
    c_recv,
):
    nx, ny, nz = dims
    nb, ng = nx * 2, ny * nz * 2
    cells = pot_in.shape[1]
    per = (cells // LANES) // nb
    share = per * LANES
    me_g = lax.axis_index("grid")
    me_b = lax.axis_index("band")
    my_x, my_h = me_b // 2, me_b % 2
    my_c, my_z, my_y = me_g % 2, (me_g // 2) % nz, me_g // (2 * nz)

    extras = [(per * nb + i, (0, nx + 1)[i]) for i in range(cells // LANES - per * nb)]
    band_offsets = [(dx, dh) for dh in (1, 0) for dx in range(nx) if (dx, dh) != (0, 0)]
    pair_offsets = [(dy, dc) for dy in range(ny) for dc in range(2) if (dy, dc) != (0, 0)]

    def band_peer(dx, dh):
        return ((my_x + dx) % nx) * 2 + (my_h + dh) % 2

    def pair_peer(dy, dc):
        return (((my_y + dy) % ny) * nz + my_z) * 2 + (my_c + dc) % 2

    def line_peer(dz):
        return (my_y * nz + (my_z + dz) % nz) * 2 + my_c

    def grid_peer(step):
        return (me_g + step + ng) % ng

    loads = [
        pltpu.make_async_copy(
            psi_in.at[b], psi.at[pl.ds(4 * b, 4), pl.ds(PAD, cells)], in_sem.at[b]
        )
        for b in range(4)
    ]
    pot_loads = [
        pltpu.make_async_copy(pot_in, pot.at[pl.ds(4 * b, 4), :], in_sem.at[4 + b])
        for b in range(2)
    ]
    for copy in loads:
        copy.start()
    for copy in pot_loads:
        copy.start()

    def table_copy(i):
        return pltpu.make_async_copy(
            table_in.at[i], table.at[pl.ds(pl.multiple_of(4 * i, 4), 4), :], table_sem.at[i]
        )

    @pl.loop(0, 48)
    def _(i):
        table_copy(i).start()

    psi[:, 0:PAD] = jnp.zeros((16, PAD), jnp.float32)
    psi[:, PAD + cells : PAD + cells + PAD] = jnp.zeros((16, PAD), jnp.float32)
    got_psi[:, share : share + LANES] = jnp.zeros((16 * nb, LANES), jnp.float32)
    got_h[:, share : share + LANES] = jnp.zeros((16 * nb, LANES), jnp.float32)

    barrier = pltpu.get_barrier_semaphore()
    peers = 0
    for dx, dh in band_offsets:
        pl.semaphore_signal(
            barrier, inc=1, device_id=(me_g, band_peer(dx, dh)), device_id_type=MESH
        )
        peers += 1
    for step in (1, -1, 2, -2):
        pl.semaphore_signal(
            barrier, inc=1, device_id=(grid_peer(step), me_b), device_id_type=MESH
        )
        peers += 1
    for dy, dc in pair_offsets:
        pl.semaphore_signal(
            barrier, inc=1, device_id=(pair_peer(dy, dc), me_b), device_id_type=MESH
        )
        peers += 1
    for dz in range(1, nz):
        pl.semaphore_signal(
            barrier, inc=1, device_id=(line_peer(dz), me_b), device_id_type=MESH
        )
        peers += 1

    _, lane = iota(8, CHUNK)
    turn = jnp.zeros((8, CHUNK), jnp.int32)
    for m in range(1, CHUNK // NY):
        turn = turn + jnp.where(lane >= m * NY, 1, 0)
    column = lane - turn * NY
    for k in range(1, 5):
        ycoef[k - 1] = jnp.where(column + k < NY, -0.5 * STENCIL[k], 0.0)
        ycoef[3 + k] = jnp.where(column >= k, -0.5 * STENCIL[k], 0.0)

    for copy in loads:
        copy.wait()
    pl.semaphore_wait(barrier, peers)

    halo = []
    for i, (step, target) in enumerate(((1, before), (-1, after))):
        copy = pltpu.make_async_remote_copy(
            src_ref=psi.at[:, pl.ds(PAD, cells)],
            dst_ref=target,
            send_sem=halo_send.at[i],
            recv_sem=halo_recv.at[i],
            device_id=(grid_peer(step), me_b),
            device_id_type=MESH,
        )
        copy.start()
        halo.append(copy)

    my_rows = pl.ds(pl.multiple_of(me_b * 16, 16), 16)

    def spread(source, base, target, send, recv, which):
        copies = []
        for i, (dx, dh) in enumerate(band_offsets):
            peer = band_peer(dx, dh)
            start = pl.multiple_of(base + peer * share, LANES)
            copy = pltpu.make_async_remote_copy(
                src_ref=source.at[:, pl.ds(start, share)],
                dst_ref=target.at[my_rows, pl.ds(0, share)],
                send_sem=send.at[i],
                recv_sem=recv.at[i],
                device_id=(me_g, peer),
                device_id_type=MESH,
            )
            copy.start()
            copies.append(copy)
        for i, (tile, owner) in enumerate(extras):

            @pl.when(me_b != owner)
            def _(i=i, tile=tile, owner=owner):
                extra_copy(source, base, target, which, i, tile, owner, me_b).start()

        return copies

    def extra_copy(source, base, target, which, i, tile, owner, sem):
        return pltpu.make_async_remote_copy(
            src_ref=source.at[:, pl.ds(base + tile * LANES, LANES)],
            dst_ref=target.at[my_rows, pl.ds(share, LANES)],
            send_sem=extra_send.at[which * 2 + i],
            recv_sem=extra_recv.at[which * 16 + sem],
            device_id=(me_g, owner),
            device_id_type=MESH,
        )

    def keep_own(source, base, target):
        start = pl.multiple_of(base + me_b * share, LANES)
        target[my_rows, 0:share] = source[:, pl.ds(start, share)]
        for tile, owner in extras:

            @pl.when(me_b == owner)
            def _(tile=tile):
                target[my_rows, share : share + LANES] = source[
                    :, base + tile * LANES : base + (tile + 1) * LANES
                ]

    def await_spread(copies, source, base, target, which):
        for copy in copies:
            copy.wait_recv()
        for i, (tile, owner) in enumerate(extras):

            @pl.when(me_b == owner)
            def _(i=i, tile=tile, owner=owner):
                for other in range(nb):
                    if other != owner:
                        extra_copy(
                            source, base, target, which, i, tile, owner, other
                        ).wait_recv()

    def await_sent(copies, source, base, target, which):
        for copy in copies:
            copy.wait_send()
        for i, (tile, owner) in enumerate(extras):

            @pl.when(me_b != owner)
            def _(i=i, tile=tile, owner=owner):
                extra_copy(source, base, target, which, i, tile, owner, me_b).wait_send()

    psi_copies = spread(psi, PAD, got_psi, psi_send, psi_recv, 0)

    @pl.loop(0, 48)
    def _(i):
        table_copy(i).wait()

    def partial_step(i, total):
        start = pl.multiple_of(i * WIDE, LANES)
        return total + dot(
            table[:, pl.ds(start, WIDE)], psi[:, pl.ds(start + PAD, WIDE)], NT
        )

    raw = lax.fori_loop(0, cells // WIDE, partial_step, jnp.zeros((192, 16), jnp.float32))
    row, col = iota(192, 16)
    raw = jnp.where((row & 3) == (col & 3), raw, 0.0)
    row, col = iota(64, 192)
    source_row = jnp.where(row < 32, row, jnp.where(row < 48, -1, row - 16))
    gather = ones_where(source_row == (col >> 2))
    row, col = iota(16, LANES)
    widen = ones_where((row >> 2) == (col >> 2))
    sums = dot(dot(gather, raw, NN), widen, NN)
    part[...] = sums
    part[32:48, :] = weight_in[...]

    part_copies = []
    for i, (step, first, count, target) in enumerate(
        ((1, 16, 48, low1), (-1, 0, 48, high1), (2, 48, 16, low2), (-2, 0, 16, high2))
    ):
        copy = pltpu.make_async_remote_copy(
            src_ref=part.at[pl.ds(first, count), :],
            dst_ref=target,
            send_sem=part_send.at[i],
            recv_sem=part_recv.at[i],
            device_id=(grid_peer(step), me_b),
            device_id_type=MESH,
        )
        copy.start()
        part_copies.append(copy)

    for copy in pot_loads:
        copy.wait()

    @pl.loop(0, cells // CHUNK)
    def _(i):
        start = pl.multiple_of(i * CHUNK, LANES)
        wide = psi[:, pl.ds(start, CHUNK + 2 * PAD)]

        def shifted(offset):
            return wide[:, PAD + offset : PAD + offset + CHUNK]

        here = pot[:, pl.ds(start, CHUNK)] + (-1.5 * STENCIL[0])
        total = jnp.concatenate([here, here], axis=0) * shifted(0)
        for k in range(1, 5):
            total = total + (-0.5 * STENCIL[k]) * (shifted(NY * k) + shifted(-NY * k))
            up, down = ycoef[k - 1], ycoef[3 + k]
            total = total + jnp.concatenate([up, up], axis=0) * shifted(k)
            total = total + jnp.concatenate([down, down], axis=0) * shifted(-k)
        h[:, pl.ds(start, CHUNK)] = total

    keep_own(psi, PAD, got_psi)

    for copy in halo:
        copy.wait_recv()
    across = z_matrix()

    @pl.loop(0, cells // WIDE)
    def _(i):
        start = pl.multiple_of(i * WIDE, LANES)
        here = pl.ds(start, WIDE)
        planes = jnp.concatenate(
            [before[:, here], psi[:, pl.ds(start + PAD, WIDE)], after[:, here]], axis=0
        )
        h[:, here] = h[:, here] + dot(across, planes, NN)

    for copy in part_copies:
        copy.wait_recv()
    coef = jnp.concatenate(
        [
            low1[16:32, :] * (low1[0:16, :] + part[0:16, :] + low2[...]),
            part[32:48, :] * (part[16:32, :] + high1[0:16, :] + low1[32:48, :]),
            high1[32:48, :] * (high1[16:32, :] + high2[...] + part[48:64, :]),
        ],
        axis=0,
    )
    row, col = iota(48, 192)
    repeat = ones_where(row == (col >> 2))
    spread_coef = dot(coef, repeat, TN)[0:16, :]
    row, col = iota(16, 192)
    spread_coef = jnp.where((row & 3) == (col & 3), spread_coef, 0.0)

    @pl.loop(0, cells // WIDE)
    def _(i):
        start = pl.multiple_of(i * WIDE, LANES)
        here = pl.ds(start, WIDE)
        h[:, here] = h[:, here] + dot(spread_coef, table[:, here], NN)

    h_copies = spread(h, 0, got_h, h_send, h_recv, 1)
    stores = [
        pltpu.make_async_copy(h.at[pl.ds(4 * b, 4), :], h_out.at[b], out_sem.at[b])
        for b in range(4)
    ]
    for copy in stores:
        copy.start()
    keep_own(h, 0, got_h)

    rows = 16 * nb
    await_spread(psi_copies, psi, PAD, got_psi, 0)
    bands = got_psi[...]
    row, col = iota(rows, rows)
    same_plane = (row & 3) == (col & 3)
    corr = jnp.where(same_plane, dot(bands, bands, NT), 0.0)
    await_spread(h_copies, h, 0, got_h, 1)
    gram = jnp.where(same_plane, dot(got_h[...], bands, NT), 0.0)
    row, col = iota(8 * nb, rows)
    band_of = (row >> 3) * 4 + (row & 3)
    pick_corr = ones_where(((row & 4) == 0) & (band_of == (col >> 2)))
    pick_gram = ones_where(((row & 4) == 4) & (band_of == (col >> 2)))
    row, col = iota(rows, LANES)
    narrow = ones_where((row >> 2) == col)
    blocks = dot(dot(pick_corr, corr, NN) + dot(pick_gram, gram, NN), narrow, NN)
    terms[...] = blocks.reshape(nb, 8, LANES)

    def exchange(source_of, target, slot, peers_, send, recv):
        copies = []
        for i, peer in enumerate(peers_):
            copy = pltpu.make_async_remote_copy(
                src_ref=source_of(i),
                dst_ref=target.at[slot],
                send_sem=send.at[i],
                recv_sem=recv.at[i],
                device_id=peer,
                device_id_type=MESH,
            )
            copy.start()
            copies.append(copy)
        return copies

    band_peers = [band_peer(dx, dh) for dx, dh in band_offsets]
    a_copies = exchange(
        lambda i: terms.at[band_peers[i]],
        band_terms,
        me_b,
        [(me_g, peer) for peer in band_peers],
        a_send,
        a_recv,
    )
    band_terms[me_b] = terms[me_b]
    for copy in a_copies:
        copy.wait_recv()
    own_sum[...] = jnp.sum(band_terms[...], axis=0)

    my_pair = my_y * 2 + my_c
    b_copies = exchange(
        lambda i: own_sum,
        pair_terms,
        my_pair,
        [(pair_peer(dy, dc), me_b) for dy, dc in pair_offsets],
        b_send,
        b_recv,
    )
    pair_terms[my_pair] = own_sum[...]
    for copy in b_copies:
        copy.wait_recv()
    pair_sum[...] = jnp.sum(pair_terms[...], axis=0)

    c_copies = exchange(
        lambda i: pair_sum,
        line_terms,
        my_z,
        [(line_peer(dz), me_b) for dz in range(1, nz)],
        c_send,
        c_recv,
    )
    line_terms[my_z] = pair_sum[...]
    for copy in c_copies:
        copy.wait_recv()
    volume = 1.0 / (4 * cells * ng)
    final = jnp.sum(line_terms[...], axis=0) * volume
    corr_out[...] = final[0:4, 0 : 4 * nb]
    gram_out[...] = final[4:8, 0 : 4 * nb]

    for copy in halo + part_copies + a_copies + b_copies + c_copies:
        copy.wait_send()
    await_sent(psi_copies, psi, PAD, got_psi, 0)
    await_sent(h_copies, h, 0, got_h, 1)
    for copy in stores:
        copy.wait()


def shards(dims, orbitals, potential, projectors, kb_energy, proj_count):
    groups, layers, cells = orbitals.shape
    nx, ny, nz = dims
    nb = nx * 2
    kinds = projectors.shape[2]
    active = lax.broadcasted_iota(jnp.int32, kb_energy.shape, 2) < proj_count[:, :, None]
    weight = jnp.where(active, kb_energy, 0.0).reshape(16, 1)
    weight = jnp.broadcast_to(weight, (16, LANES))
    width = ((cells // LANES) // nb + 1) * LANES
    f32 = jnp.float32
    any_space = pl.BlockSpec(memory_space=pl.ANY)
    vmem = pl.BlockSpec(memory_space=pltpu.VMEM)
    dma = pltpu.SemaphoreType.DMA
    return pl.pallas_call(
        functools.partial(kernel, dims),
        out_shape=(
            jax.ShapeDtypeStruct(orbitals.shape, f32),
            jax.ShapeDtypeStruct((groups, groups * nb), f32),
            jax.ShapeDtypeStruct((groups, groups * nb), f32),
        ),
        in_specs=[any_space, any_space, any_space, vmem],
        out_specs=(any_space, vmem, vmem),
        scratch_shapes=[
            pltpu.VMEM((16, cells + 2 * PAD), f32),
            pltpu.VMEM((16, cells), f32),
            pltpu.VMEM((16, cells), f32),
            pltpu.VMEM((8, cells), f32),
            pltpu.VMEM((192, cells), f32),
            pltpu.VMEM((16, cells), f32),
            pltpu.VMEM((16 * nb, width), f32),
            pltpu.VMEM((16 * nb, width), f32),
            pltpu.VMEM((8, 8, CHUNK), f32),
            pltpu.VMEM((64, LANES), f32),
            pltpu.VMEM((48, LANES), f32),
            pltpu.VMEM((48, LANES), f32),
            pltpu.VMEM((16, LANES), f32),
            pltpu.VMEM((16, LANES), f32),
            pltpu.VMEM((nb, 8, LANES), f32),
            pltpu.VMEM((nb, 8, LANES), f32),
            pltpu.VMEM((8, LANES), f32),
            pltpu.VMEM((ny * 2, 8, LANES), f32),
            pltpu.VMEM((8, LANES), f32),
            pltpu.VMEM((nz, 8, LANES), f32),
            dma((6,)),
            dma((48,)),
            dma((2,)),
            dma((2,)),
            dma((4,)),
            dma((4,)),
            dma((nb,)),
            dma((nb,)),
            dma((nb,)),
            dma((nb,)),
            dma((4,)),
            dma((32,)),
            dma((4,)),
            dma((nb,)),
            dma((nb,)),
            dma((ny * 2,)),
            dma((ny * 2,)),
            dma((nz,)),
            dma((nz,)),
        ],
        compiler_params=pltpu.CompilerParams(
            collective_id=0, has_side_effects=True, vmem_limit_bytes=60 * 2**20
        ),
        cost_estimate=pl.CostEstimate(
            flops=80_000_000, bytes_accessed=6_000_000, transcendentals=0
        ),
    )(
        orbitals,
        potential,
        projectors.reshape(3 * 2 * kinds, layers, cells),
        weight,
    )


def solution(mesh):
    ny = 4 if mesh.shape["grid"] == 64 else 1
    dims = (mesh.shape["band"] // 2, ny, mesh.shape["grid"] // (2 * ny))
    in_specs = (
        P("band", "grid", None),
        P("grid", None),
        P(None, None, None, "grid", None),
        P("grid", None, None),
        P("grid", None),
    )
    out_specs = (P("band", "grid", None), P("band", None), P("band", None))
    return jax.shard_map(
        functools.partial(shards, dims),
        mesh=mesh,
        in_specs=in_specs,
        out_specs=out_specs,
        check_vma=False,
    )
```

time: 524 us -> 84.2 us (0.16); the launches traced: 514 us -> 83.9 us
  blocking collectives: 436 us -> 0 us
  Pallas kernels: 0 us -> 77.5 us
  matrix products: 26 us -> 0 us
  starting transfers between devices: 19.6 us -> 0 us
  between operations: 14.2 us -> 0.64 us
  local copies, waits for them, and re-layouts: 16.4 us -> 5.04 us
    psum x2 -> x0, blocking collectives: 436 us -> none  [the longest x1 293 us: shards(): summed = lax.psum(spread, 'grid')]
    pallas_call x0 -> x1, Pallas kernels: none -> 77.5 us  [shards(): pl.pallas_call(functools.partial(kernel, dims), out_shape=(jax.ShapeDtype...]
    dot_general x4 -> x0, matrix products: 26 us -> none  [the longest x3 18.3 us: contract_rows(): lax.dot_general(first_mat, second_mat, (((1,), (1,)), ((), ())), precisio...]
    ppermute x4 -> x0, starting transfers between devices: 19.5 us -> none  [the longest x2 14 us: extended(): lax.ppermute(lax.slice_in_dim(block, 0, width, axis=dim), axis, backward)]
    unnamed x18 -> x3, local copies, waits for them, and re-layouts: 15.9 us -> 4.28 us
  transfers between devices with their start and end apart: 5 -> 0, of which waited for: 1 -> 0; matrix products, arithmetic and copies ran while one was open for 4% -> 0% of each run, Pallas kernels for 0% -> 0%
where the time goes in v1:
time: 84.2 us; the launch traced here: 83.9 us
  Pallas kernels  77.5 us (92%)
  local copies, waits for them, and re-layouts  5.04 us (6%)
    pallas_call x1, Pallas kernels, shards(): pl.pallas_call(functools.partial(kernel, dims), out_shape=(jax.ShapeDtype...  77.5 us
    unnamed x3, local copies, waits for them, and re-layouts  4.28 us

profile of v1, /device:TPU:1, one launch (start us, length us, event | category | flops | bytes accessed | tf_op | source)
XLA Modules:
  0.0 83.9 jit_solution(816339219929053514)
XLA Ops:
  0.6 0.8 compare_select_fusion
  1.4 0.1 broadcast_in_dim.13
  1.5 0.7 broadcast_in_dim.14.weight_in
  2.1 77.5 %shard_map.79 = (f32[4,4,6400]{2,1,0:T(4,128)}, f32[4,64]{1,0:T(4,128)}, f32[4,64]{1,0:T(4,128)}) custom-call(f32[4,4,6400]{2,1,0:T(4,128)} %psi_in.1, f32[4,6400]{1,0:T(4,128)} %pot_in.1, f32[48,4,6400]{2,1,0:T(4,128)} %bitcast.2, f32[16,128]{1,0:T(8,128)} %broadcast_in_dim.14.weight_in), custom_call_target="tpu_custom_call" | custom-call | flops 80000000 | bytes 6000000 | tf_op jit(solution)/shard_map/pallas_call | solution.py:479
  79.7 1.8 %copy.11 = f32[4,4,6400]{2,1,0:T(4,128)} copy(f32[4,4,6400]{2,1,0:T(4,128)} %get-tuple-element.6) | data formatting | bytes 819200
  81.4 1.3 %copy.12 = f32[4,64]{1,0:T(4,128)} copy(f32[4,64]{1,0:T(4,128)} %get-tuple-element.7) | data formatting | bytes 2048
  82.7 1.2 %copy.13 = f32[4,64]{1,0:T(4,128)} copy(f32[4,64]{1,0:T(4,128)} %get-tuple-element.8) | data formatting | bytes 2048

commit v2 on v1

--- a/solution.py
+++ b/solution.py
@@ -58,16 +58,19 @@
     psi_in,
     pot_in,
     table_in,
-    weight_in,
+    energy_in,
+    count_in,
     h_out,
-    corr_out,
-    gram_out,
+    sums_out,
     psi,
     before,
     after,
     pot,
     table,
+    energy,
+    count,
     h,
+    full,
     got_psi,
     got_h,
     ycoef,
@@ -76,12 +79,14 @@
     high1,
     low2,
     high2,
+    owner,
+    owners,
     terms,
-    band_terms,
-    own_sum,
-    pair_terms,
-    pair_sum,
-    line_terms,
+    x_terms,
+    x_sum,
+    y_terms,
+    y_sum,
+    z_terms,
     in_sem,
     table_sem,
     halo_send,
@@ -94,13 +99,15 @@
     h_recv,
     extra_send,
     extra_recv,
+    owner_send,
+    owner_recv,
     out_sem,
-    a_send,
-    a_recv,
-    b_send,
-    b_recv,
-    c_send,
-    c_recv,
+    x_send,
+    x_recv,
+    y_send,
+    y_recv,
+    z_send,
+    z_recv,
 ):
     nx, ny, nz = dims
     nb, ng = nx * 2, ny * nz * 2
@@ -114,16 +121,20 @@
 
     extras = [(per * nb + i, (0, nx + 1)[i]) for i in range(cells // LANES - per * nb)]
     band_offsets = [(dx, dh) for dh in (1, 0) for dx in range(nx) if (dx, dh) != (0, 0)]
-    pair_offsets = [(dy, dc) for dy in range(ny) for dc in range(2) if (dy, dc) != (0, 0)]
+    x_offsets = range(1, nx)
+    y_offsets = [(dh, dy) for dh in (1, 0) for dy in range(ny) if (dh, dy) != (0, 0)]
+    z_offsets = [(dz, dc) for dz in range(nz) for dc in range(2) if (dz, dc) != (0, 0)]
+    root = me_g % nb
 
     def band_peer(dx, dh):
         return ((my_x + dx) % nx) * 2 + (my_h + dh) % 2
 
-    def pair_peer(dy, dc):
-        return (((my_y + dy) % ny) * nz + my_z) * 2 + (my_c + dc) % 2
-
-    def line_peer(dz):
-        return (my_y * nz + (my_z + dz) % nz) * 2 + my_c
+    def y_peer(dh, dy):
+        peer_g = (((my_y + dy) % ny) * nz + my_z) * 2 + my_c
+        return peer_g, my_x * 2 + (my_h + dh) % 2
+
+    def z_peer(dz, dc):
+        return (my_y * nz + (my_z + dz) % nz) * 2 + (my_c + dc) % 2, me_b
 
     def grid_peer(step):
         return (me_g + step + ng) % ng
@@ -140,7 +151,11 @@
     ]
     for copy in loads:
         copy.start()
-    for copy in pot_loads:
+    small_loads = pot_loads + [
+        pltpu.make_async_copy(energy_in, energy, in_sem.at[6]),
+        pltpu.make_async_copy(count_in, count, in_sem.at[7]),
+    ]
+    for copy in small_loads:
         copy.start()
 
     def table_copy(i):
@@ -156,6 +171,7 @@
     psi[:, PAD + cells : PAD + cells + PAD] = jnp.zeros((16, PAD), jnp.float32)
     got_psi[:, share : share + LANES] = jnp.zeros((16 * nb, LANES), jnp.float32)
     got_h[:, share : share + LANES] = jnp.zeros((16 * nb, LANES), jnp.float32)
+    owners[...] = jnp.zeros(owners.shape, jnp.float32)
 
     barrier = pltpu.get_barrier_semaphore()
     peers = 0
@@ -169,15 +185,10 @@
             barrier, inc=1, device_id=(grid_peer(step), me_b), device_id_type=MESH
         )
         peers += 1
-    for dy, dc in pair_offsets:
-        pl.semaphore_signal(
-            barrier, inc=1, device_id=(pair_peer(dy, dc), me_b), device_id_type=MESH
-        )
-        peers += 1
-    for dz in range(1, nz):
-        pl.semaphore_signal(
-            barrier, inc=1, device_id=(line_peer(dz), me_b), device_id_type=MESH
-        )
+    for peer in [y_peer(dh, dy) for dh, dy in y_offsets] + [
+        z_peer(dz, dc) for dz, dc in z_offsets
+    ]:
+        pl.semaphore_signal(barrier, inc=1, device_id=peer, device_id_type=MESH)
         peers += 1
 
     _, lane = iota(8, CHUNK)
@@ -296,7 +307,18 @@
     widen = ones_where((row >> 2) == (col >> 2))
     sums = dot(dot(gather, raw, NN), widen, NN)
     part[...] = sums
-    part[32:48, :] = weight_in[...]
+    for copy in small_loads:
+        copy.wait()
+    row, col = iota(16, 8)
+    kinds = jnp.concatenate(
+        [jnp.broadcast_to(energy[0, a : a + 1, :], (8, 8)) for a in range(2)], axis=0
+    )
+    active = jnp.concatenate(
+        [jnp.broadcast_to(count[0:1, a : a + 1], (8, 8)) for a in range(2)], axis=0
+    )
+    chosen = jnp.where((col == (row & 7)) & (col < active), kinds, 0.0)
+    weight = jnp.broadcast_to(jnp.sum(chosen, axis=1, keepdims=True), (16, LANES))
+    part[32:48, :] = weight
 
     part_copies = []
     for i, (step, first, count, target) in enumerate(
@@ -313,9 +335,6 @@
         copy.start()
         part_copies.append(copy)
 
-    for copy in pot_loads:
-        copy.wait()
-
     @pl.loop(0, cells // CHUNK)
     def _(i):
         start = pl.multiple_of(i * CHUNK, LANES)
@@ -348,16 +367,43 @@
         )
         h[:, here] = h[:, here] + dot(across, planes, NN)
 
+    h_copies = spread(h, 0, got_h, h_send, h_recv, 1)
+    keep_own(h, 0, got_h)
+
     for copy in part_copies:
         copy.wait_recv()
+    total = part[16:32, :] + high1[0:16, :] + low1[32:48, :]
     coef = jnp.concatenate(
         [
             low1[16:32, :] * (low1[0:16, :] + part[0:16, :] + low2[...]),
-            part[32:48, :] * (part[16:32, :] + high1[0:16, :] + low1[32:48, :]),
+            weight * total,
             high1[32:48, :] * (high1[16:32, :] + high2[...] + part[48:64, :]),
         ],
         axis=0,
     )
+
+    row, col = iota(LANES, LANES)
+    place = ones_where((row < 16) & ((row & 3) == 0) & (col == me_b * 4 + (row >> 2)))
+    owner[...] = dot(total, place, NN)
+
+    def owner_copy(sem):
+        return pltpu.make_async_remote_copy(
+            src_ref=owner,
+            dst_ref=owners.at[me_b],
+            send_sem=owner_send,
+            recv_sem=owner_recv.at[sem],
+            device_id=(me_g, root),
+            device_id_type=MESH,
+        )
+
+    @pl.when(me_b != root)
+    def _():
+        owner_copy(me_b).start()
+
+    @pl.when(me_b == root)
+    def _():
+        owners[me_b] = owner[...]
+
     row, col = iota(48, 192)
     repeat = ones_where(row == (col >> 2))
     spread_coef = dot(coef, repeat, TN)[0:16, :]
@@ -368,32 +414,45 @@
     def _(i):
         start = pl.multiple_of(i * WIDE, LANES)
         here = pl.ds(start, WIDE)
-        h[:, here] = h[:, here] + dot(spread_coef, table[:, here], NN)
-
-    h_copies = spread(h, 0, got_h, h_send, h_recv, 1)
+        full[:, here] = h[:, here] + dot(spread_coef, table[:, here], NN)
+
     stores = [
-        pltpu.make_async_copy(h.at[pl.ds(4 * b, 4), :], h_out.at[b], out_sem.at[b])
+        pltpu.make_async_copy(full.at[pl.ds(4 * b, 4), :], h_out.at[b], out_sem.at[b])
         for b in range(4)
     ]
     for copy in stores:
         copy.start()
-    keep_own(h, 0, got_h)
+
+    @pl.when(me_b == root)
+    def _():
+        for other in range(nb):
+
+            @pl.when(other != me_b)
+            def _(other=other):
+                owner_copy(other).wait_recv()
+
+    projections = jnp.sum(owners[...], axis=0)
+    nonlocal_gram = dot(projections * weight, projections, TN)
 
     rows = 16 * nb
-    await_spread(psi_copies, psi, PAD, got_psi, 0)
-    bands = got_psi[...]
-    row, col = iota(rows, rows)
-    same_plane = (row & 3) == (col & 3)
-    corr = jnp.where(same_plane, dot(bands, bands, NT), 0.0)
-    await_spread(h_copies, h, 0, got_h, 1)
-    gram = jnp.where(same_plane, dot(got_h[...], bands, NT), 0.0)
     row, col = iota(8 * nb, rows)
     band_of = (row >> 3) * 4 + (row & 3)
     pick_corr = ones_where(((row & 4) == 0) & (band_of == (col >> 2)))
     pick_gram = ones_where(((row & 4) == 4) & (band_of == (col >> 2)))
+    row, col = iota(8 * nb, LANES)
+    band_of = (row >> 3) * 4 + (row & 3)
+    pick_nonlocal = ones_where(((row & 4) == 4) & (band_of == col))
     row, col = iota(rows, LANES)
     narrow = ones_where((row >> 2) == col)
-    blocks = dot(dot(pick_corr, corr, NN) + dot(pick_gram, gram, NN), narrow, NN)
+    row, col = iota(rows, rows)
+    same_plane = (row & 3) == (col & 3)
+    await_spread(psi_copies, psi, PAD, got_psi, 0)
+    bands = got_psi[...]
+    corr = jnp.where(same_plane, dot(bands, bands, NT), 0.0)
+    early = dot(pick_nonlocal, nonlocal_gram, NN) + dot(dot(pick_corr, corr, NN), narrow, NN)
+    await_spread(h_copies, h, 0, got_h, 1)
+    gram = jnp.where(same_plane, dot(got_h[...], bands, NT), 0.0)
+    blocks = early + dot(dot(pick_gram, gram, NN), narrow, NN)
     terms[...] = blocks.reshape(nb, 8, LANES)
 
     def exchange(source_of, target, slot, peers_, send, recv):
@@ -411,55 +470,68 @@
             copies.append(copy)
         return copies
 
-    band_peers = [band_peer(dx, dh) for dx, dh in band_offsets]
-    a_copies = exchange(
-        lambda i: terms.at[band_peers[i]],
-        band_terms,
-        me_b,
-        [(me_g, peer) for peer in band_peers],
-        a_send,
-        a_recv,
-    )
-    band_terms[me_b] = terms[me_b]
-    for copy in a_copies:
+    x_copies = exchange(
+        lambda i: terms.at[pl.ds(((my_x + x_offsets[i]) % nx) * 2, 2)],
+        x_terms,
+        my_x,
+        [(me_g, band_peer(dx, 0)) for dx in x_offsets],
+        x_send,
+        x_recv,
+    )
+    x_terms[my_x] = terms[pl.ds(my_x * 2, 2)]
+    for copy in x_copies:
         copy.wait_recv()
-    own_sum[...] = jnp.sum(band_terms[...], axis=0)
-
-    my_pair = my_y * 2 + my_c
-    b_copies = exchange(
-        lambda i: own_sum,
-        pair_terms,
-        my_pair,
-        [(pair_peer(dy, dc), me_b) for dy, dc in pair_offsets],
-        b_send,
-        b_recv,
-    )
-    pair_terms[my_pair] = own_sum[...]
-    for copy in b_copies:
+    x_sum[...] = jnp.sum(x_terms[...], axis=0)
+
+    slot = my_h * ny + my_y
+    y_copies = exchange(
+        lambda i: x_sum.at[(my_h + y_offsets[i][0]) % 2],
+        y_terms,
+        slot,
+        [y_peer(dh, dy) for dh, dy in y_offsets],
+        y_send,
+        y_recv,
+    )
+    y_terms[slot] = x_sum[my_h]
+    for copy in y_copies:
         copy.wait_recv()
-    pair_sum[...] = jnp.sum(pair_terms[...], axis=0)
-
-    c_copies = exchange(
-        lambda i: pair_sum,
-        line_terms,
-        my_z,
-        [(line_peer(dz), me_b) for dz in range(1, nz)],
-        c_send,
-        c_recv,
-    )
-    line_terms[my_z] = pair_sum[...]
-    for copy in c_copies:
+    y_sum[...] = jnp.sum(y_terms[...], axis=0)
+
+    slot = my_z * 2 + my_c
+    z_copies = exchange(
+        lambda i: y_sum,
+        z_terms,
+        slot,
+        [z_peer(dz, dc) for dz, dc in z_offsets],
+        z_send,
+        z_recv,
+    )
+    z_terms[slot] = y_sum[...]
+    for copy in z_copies:
         copy.wait_recv()
-    volume = 1.0 / (4 * cells * ng)
-    final = jnp.sum(line_terms[...], axis=0) * volume
-    corr_out[...] = final[0:4, 0 : 4 * nb]
-    gram_out[...] = final[4:8, 0 : 4 * nb]
-
-    for copy in halo + part_copies + a_copies + b_copies + c_copies:
+    sums_out[...] = jnp.sum(z_terms[...], axis=0) * (1.0 / (4 * cells * ng))
+
+    for copy in halo + part_copies + x_copies + y_copies + z_copies:
         copy.wait_send()
     await_sent(psi_copies, psi, PAD, got_psi, 0)
     await_sent(h_copies, h, 0, got_h, 1)
+
+    @pl.when(me_b != root)
+    def _():
+        owner_copy(me_b).wait_send()
+
     for copy in stores:
+        copy.wait()
+
+
+def finish(h_in, sums_in, h_out, corr_out, gram_out, sem):
+    copies = [pltpu.make_async_copy(h_in.at[b], h_out.at[b], sem.at[b]) for b in range(4)]
+    for copy in copies:
+        copy.start()
+    width = corr_out.shape[1]
+    corr_out[...] = sums_in[0:4, 0:width]
+    gram_out[...] = sums_in[4:8, 0:width]
+    for copy in copies:
         copy.wait()
 
 
@@ -468,29 +540,28 @@
     nx, ny, nz = dims
     nb = nx * 2
     kinds = projectors.shape[2]
-    active = lax.broadcasted_iota(jnp.int32, kb_energy.shape, 2) < proj_count[:, :, None]
-    weight = jnp.where(active, kb_energy, 0.0).reshape(16, 1)
-    weight = jnp.broadcast_to(weight, (16, LANES))
     width = ((cells // LANES) // nb + 1) * LANES
     f32 = jnp.float32
     any_space = pl.BlockSpec(memory_space=pl.ANY)
     vmem = pl.BlockSpec(memory_space=pltpu.VMEM)
     dma = pltpu.SemaphoreType.DMA
-    return pl.pallas_call(
+    full, sums = pl.pallas_call(
         functools.partial(kernel, dims),
         out_shape=(
             jax.ShapeDtypeStruct(orbitals.shape, f32),
-            jax.ShapeDtypeStruct((groups, groups * nb), f32),
-            jax.ShapeDtypeStruct((groups, groups * nb), f32),
+            jax.ShapeDtypeStruct((8, LANES), f32),
         ),
-        in_specs=[any_space, any_space, any_space, vmem],
-        out_specs=(any_space, vmem, vmem),
+        in_specs=[any_space] * 5,
+        out_specs=(any_space, vmem),
         scratch_shapes=[
             pltpu.VMEM((16, cells + 2 * PAD), f32),
             pltpu.VMEM((16, cells), f32),
             pltpu.VMEM((16, cells), f32),
             pltpu.VMEM((8, cells), f32),
             pltpu.VMEM((192, cells), f32),
+            pltpu.VMEM(kb_energy.shape, f32),
+            pltpu.VMEM(proj_count.shape, jnp.int32),
+            pltpu.VMEM((16, cells), f32),
             pltpu.VMEM((16, cells), f32),
             pltpu.VMEM((16 * nb, width), f32),
             pltpu.VMEM((16 * nb, width), f32),
@@ -500,13 +571,15 @@
             pltpu.VMEM((48, LANES), f32),
             pltpu.VMEM((16, LANES), f32),
             pltpu.VMEM((16, LANES), f32),
+            pltpu.VMEM((16, LANES), f32),
+            pltpu.VMEM((nb, 16, LANES), f32),
             pltpu.VMEM((nb, 8, LANES), f32),
-            pltpu.VMEM((nb, 8, LANES), f32),
-            pltpu.VMEM((8, LANES), f32),
+            pltpu.VMEM((nx, 2, 8, LANES), f32),
+            pltpu.VMEM((2, 8, LANES), f32),
             pltpu.VMEM((ny * 2, 8, LANES), f32),
             pltpu.VMEM((8, LANES), f32),
-            pltpu.VMEM((nz, 8, LANES), f32),
-            dma((6,)),
+            pltpu.VMEM((nz * 2, 8, LANES), f32),
+            dma((8,)),
             dma((48,)),
             dma((2,)),
             dma((2,)),
@@ -518,13 +591,15 @@
             dma((nb,)),
             dma((4,)),
             dma((32,)),
+            dma,
+            dma((nb,)),
             dma((4,)),
-            dma((nb,)),
-            dma((nb,)),
+            dma((nx,)),
+            dma((nx,)),
             dma((ny * 2,)),
             dma((ny * 2,)),
-            dma((nz,)),
-            dma((nz,)),
+            dma((nz * 2,)),
+            dma((nz * 2,)),
         ],
         compiler_params=pltpu.CompilerParams(
             collective_id=0, has_side_effects=True, vmem_limit_bytes=60 * 2**20
@@ -536,8 +611,22 @@
         orbitals,
         potential,
         projectors.reshape(3 * 2 * kinds, layers, cells),
-        weight,
-    )
+        kb_energy,
+        proj_count,
+    )
+    return pl.pallas_call(
+        finish,
+        out_shape=(
+            jax.ShapeDtypeStruct(orbitals.shape, f32),
+            jax.ShapeDtypeStruct((groups, groups * nb), f32),
+            jax.ShapeDtypeStruct((groups, groups * nb), f32),
+        ),
+        in_specs=[any_space, vmem],
+        out_specs=(any_space, vmem, vmem),
+        scratch_shapes=[dma((4,))],
+        compiler_params=pltpu.CompilerParams(vmem_limit_bytes=60 * 2**20),
+        cost_estimate=pl.CostEstimate(flops=0, bytes_accessed=900_000, transcendentals=0),
+    )(full, sums)
 
 
 def solution(mesh):

time: 84.2 us -> 93.7 us (1.11)
  Pallas kernels: 77.5 us -> 92.9 us
  local copies, waits for them, and re-layouts: 5.04 us -> 0 us
    pallas_call x0 -> x1, Pallas kernels: none -> 14.8 us  [shards(): pl.pallas_call(finish, out_shape=(jax.ShapeDtypeStruct(orbitals.shape, f3...]
    unnamed x3 -> x0, local copies, waits for them, and re-layouts: 4.28 us -> none
where the time goes in v2:
time: 93.7 us; the launch traced here: 93.5 us
  Pallas kernels  92.9 us (99%)
    pallas_call x1, Pallas kernels, shards(): pl.pallas_call(functools.partial(kernel, dims), out_shape=(jax.ShapeDtype...  78.1 us
    pallas_call x1, Pallas kernels, shards(): pl.pallas_call(finish, out_shape=(jax.ShapeDtypeStruct(orbitals.shape, f3...  14.8 us

profile of v2, /device:TPU:1, one launch (start us, length us, event | category | flops | bytes accessed | tf_op | source)
XLA Modules:
  0.0 93.5 jit_solution(9803907218013513770)
XLA Ops:
  0.6 78.1 %shard_map.76 = (f32[4,4,6400]{2,1,0:T(4,128)}, f32[8,128]{1,0:T(8,128)}) custom-call(f32[4,4,6400]{2,1,0:T(4,128)} %psi_in.1, f32[4,6400]{1,0:T(4,128)} %pot_in.1, f32[48,4,6400]{2,1,0:T(4,128)} %bitcast.1, f32[1,2,8]{2,1,0:T(2,128)} %energy_in.1, s32[1,2]{1,0:T(1,128)} %count_in.1), custom_call_target="tpu_custom_call" | custom-call | flops 80000000 | bytes 6000000 | tf_op jit(solution)/shard_map/pallas_call | solution.py:548
  78.7 14.8 %shard_map.77 = (f32[4,4,6400]{2,1,0:T(4,128)}, f32[4,64]{1,0:T(4,128)}, f32[4,64]{1,0:T(4,128)}) custom-call(f32[4,4,6400]{2,1,0:T(4,128)} %get-tuple-element.5.h_in, f32[8,128]{1,0:T(8,128)} %get-tuple-element.6.sums_in), custom_call_target="tpu_custom_call" | custom-call | bytes 900000 | tf_op jit(solution)/shard_map/pallas_call | solution.py:617

commit v3 on v2

--- a/solution.py
+++ b/solution.py
@@ -139,6 +139,24 @@
     def grid_peer(step):
         return (me_g + step + ng) % ng
 
+    barrier = pltpu.get_barrier_semaphore()
+    peers = 0
+    for dx, dh in band_offsets:
+        pl.semaphore_signal(
+            barrier, inc=1, device_id=(me_g, band_peer(dx, dh)), device_id_type=MESH
+        )
+        peers += 1
+    for step in (1, -1, 2, -2):
+        pl.semaphore_signal(
+            barrier, inc=1, device_id=(grid_peer(step), me_b), device_id_type=MESH
+        )
+        peers += 1
+    for peer in [y_peer(dh, dy) for dh, dy in y_offsets] + [
+        z_peer(dz, dc) for dz, dc in z_offsets
+    ]:
+        pl.semaphore_signal(barrier, inc=1, device_id=peer, device_id_type=MESH)
+        peers += 1
+
     loads = [
         pltpu.make_async_copy(
             psi_in.at[b], psi.at[pl.ds(4 * b, 4), pl.ds(PAD, cells)], in_sem.at[b]
@@ -169,27 +187,16 @@
 
     psi[:, 0:PAD] = jnp.zeros((16, PAD), jnp.float32)
     psi[:, PAD + cells : PAD + cells + PAD] = jnp.zeros((16, PAD), jnp.float32)
-    got_psi[:, share : share + LANES] = jnp.zeros((16 * nb, LANES), jnp.float32)
-    got_h[:, share : share + LANES] = jnp.zeros((16 * nb, LANES), jnp.float32)
-    owners[...] = jnp.zeros(owners.shape, jnp.float32)
-
-    barrier = pltpu.get_barrier_semaphore()
-    peers = 0
-    for dx, dh in band_offsets:
-        pl.semaphore_signal(
-            barrier, inc=1, device_id=(me_g, band_peer(dx, dh)), device_id_type=MESH
-        )
-        peers += 1
-    for step in (1, -1, 2, -2):
-        pl.semaphore_signal(
-            barrier, inc=1, device_id=(grid_peer(step), me_b), device_id_type=MESH
-        )
-        peers += 1
-    for peer in [y_peer(dh, dy) for dh, dy in y_offsets] + [
-        z_peer(dz, dc) for dz, dc in z_offsets
-    ]:
-        pl.semaphore_signal(barrier, inc=1, device_id=peer, device_id_type=MESH)
-        peers += 1
+
+    @pl.when((me_b != extras[0][1]) & (me_b != extras[1][1]))
+    def _():
+        got_psi[:, share : share + LANES] = jnp.zeros((16 * nb, LANES), jnp.float32)
+        got_h[:, share : share + LANES] = jnp.zeros((16 * nb, LANES), jnp.float32)
+
+    @pl.when(me_b != root)
+    def _():
+        owners[...] = jnp.zeros(owners.shape, jnp.float32)
+
 
     _, lane = iota(8, CHUNK)
     turn = jnp.zeros((8, CHUNK), jnp.int32)
@@ -524,14 +531,18 @@
         copy.wait()
 
 
-def finish(h_in, sums_in, h_out, corr_out, gram_out, sem):
-    copies = [pltpu.make_async_copy(h_in.at[b], h_out.at[b], sem.at[b]) for b in range(4)]
-    for copy in copies:
+def finish(h_in, sums_in, h_out, corr_out, gram_out, held, sem):
+    ins = [pltpu.make_async_copy(h_in.at[b], held.at[b], sem.at[b]) for b in range(4)]
+    outs = [pltpu.make_async_copy(held.at[b], h_out.at[b], sem.at[4 + b]) for b in range(4)]
+    for copy in ins:
         copy.start()
     width = corr_out.shape[1]
     corr_out[...] = sums_in[0:4, 0:width]
     gram_out[...] = sums_in[4:8, 0:width]
-    for copy in copies:
+    for copy, onward in zip(ins, outs):
+        copy.wait()
+        onward.start()
+    for copy in outs:
         copy.wait()
 
 
@@ -623,7 +634,7 @@
         ),
         in_specs=[any_space, vmem],
         out_specs=(any_space, vmem, vmem),
-        scratch_shapes=[dma((4,))],
+        scratch_shapes=[pltpu.VMEM(orbitals.shape, f32), dma((8,))],
         compiler_params=pltpu.CompilerParams(vmem_limit_bytes=60 * 2**20),
         cost_estimate=pl.CostEstimate(flops=0, bytes_accessed=900_000, transcendentals=0),
     )(full, sums)

time: 93.7 us -> 81.2 us (0.87)
  Pallas kernels: 92.9 us -> 80.4 us
    pallas_call x1, Pallas kernels: 14.8 us -> 3.02 us  [shards(): pl.pallas_call(finish, out_shape=(jax.ShapeDtypeStruct(orbitals.shape, f3...]
where the time goes in v3:
time: 81.2 us; the launch traced here: 81 us
  Pallas kernels  80.4 us (99%)
    pallas_call x1, Pallas kernels, shards(): pl.pallas_call(functools.partial(kernel, dims), out_shape=(jax.ShapeDtype...  77.3 us
    pallas_call x1, Pallas kernels, shards(): pl.pallas_call(finish, out_shape=(jax.ShapeDtypeStruct(orbitals.shape, f3...  3.02 us

profile of v3, /device:TPU:1, one launch (start us, length us, event | category | flops | bytes accessed | tf_op | source)
XLA Modules:
  0.0 81.0 jit_solution(4751555294271643467)
XLA Ops:
  0.6 77.3 %shard_map.76 = (f32[4,4,6400]{2,1,0:T(4,128)}, f32[8,128]{1,0:T(8,128)}) custom-call(f32[4,4,6400]{2,1,0:T(4,128)} %psi_in.1, f32[4,6400]{1,0:T(4,128)} %pot_in.1, f32[48,4,6400]{2,1,0:T(4,128)} %bitcast.1, f32[1,2,8]{2,1,0:T(2,128)} %energy_in.1, s32[1,2]{1,0:T(1,128)} %count_in.1), custom_call_target="tpu_custom_call" | custom-call | flops 80000000 | bytes 6000000 | tf_op jit(solution)/shard_map/pallas_call | solution.py:559
  78.0 3.0 %shard_map.77 = (f32[4,4,6400]{2,1,0:T(4,128)}, f32[4,64]{1,0:T(4,128)}, f32[4,64]{1,0:T(4,128)}) custom-call(f32[4,4,6400]{2,1,0:T(4,128)} %get-tuple-element.5.h_in, f32[8,128]{1,0:T(8,128)} %get-tuple-element.6.sums_in), custom_call_target="tpu_custom_call" | custom-call | bytes 900000 | tf_op jit(solution)/shard_map/pallas_call | solution.py:628

commit v4 on v3

--- a/solution.py
+++ b/solution.py
@@ -73,6 +73,7 @@
     full,
     got_psi,
     got_h,
+    got_next,
     ycoef,
     part,
     low1,
@@ -99,6 +100,8 @@
     h_recv,
     extra_send,
     extra_recv,
+    next_send,
+    next_recv,
     owner_send,
     owner_recv,
     out_sem,
@@ -120,10 +123,12 @@
     my_c, my_z, my_y = me_g % 2, (me_g // 2) % nz, me_g // (2 * nz)
 
     extras = [(per * nb + i, (0, nx + 1)[i]) for i in range(cells // LANES - per * nb)]
-    band_offsets = [(dx, dh) for dh in (1, 0) for dx in range(nx) if (dx, dh) != (0, 0)]
-    x_offsets = range(1, nx)
+    far_x = sorted(range(nx), key=lambda dx: -min(dx, nx - dx))
+    far_z = sorted(range(nz), key=lambda dz: -min(dz, nz - dz))
+    band_offsets = [(dx, dh) for dh in (1, 0) for dx in far_x if (dx, dh) != (0, 0)]
+    x_offsets = [dx for dx in far_x if dx]
     y_offsets = [(dh, dy) for dh in (1, 0) for dy in range(ny) if (dh, dy) != (0, 0)]
-    z_offsets = [(dz, dc) for dz in range(nz) for dc in range(2) if (dz, dc) != (0, 0)]
+    z_offsets = [(dz, dc) for dz in far_z for dc in (1, 0) if (dz, dc) != (0, 0)]
     root = me_g % nb
 
     def band_peer(dx, dh):
@@ -192,6 +197,7 @@
     def _():
         got_psi[:, share : share + LANES] = jnp.zeros((16 * nb, LANES), jnp.float32)
         got_h[:, share : share + LANES] = jnp.zeros((16 * nb, LANES), jnp.float32)
+        got_next[:, share : share + LANES] = jnp.zeros((16 * nb, LANES), jnp.float32)
 
     @pl.when(me_b != root)
     def _():
@@ -210,19 +216,6 @@
     for copy in loads:
         copy.wait()
     pl.semaphore_wait(barrier, peers)
-
-    halo = []
-    for i, (step, target) in enumerate(((1, before), (-1, after))):
-        copy = pltpu.make_async_remote_copy(
-            src_ref=psi.at[:, pl.ds(PAD, cells)],
-            dst_ref=target,
-            send_sem=halo_send.at[i],
-            recv_sem=halo_recv.at[i],
-            device_id=(grid_peer(step), me_b),
-            device_id_type=MESH,
-        )
-        copy.start()
-        halo.append(copy)
 
     my_rows = pl.ds(pl.multiple_of(me_b * 16, 16), 16)
 
@@ -294,6 +287,44 @@
 
     psi_copies = spread(psi, PAD, got_psi, psi_send, psi_recv, 0)
 
+    halo = []
+    for i, (step, target) in enumerate(((1, before), (-1, after))):
+        copy = pltpu.make_async_remote_copy(
+            src_ref=psi.at[:, pl.ds(PAD, cells)],
+            dst_ref=target,
+            send_sem=halo_send.at[i],
+            recv_sem=halo_recv.at[i],
+            device_id=(grid_peer(step), me_b),
+            device_id_type=MESH,
+        )
+        copy.start()
+        halo.append(copy)
+
+    for copy in small_loads:
+        copy.wait()
+
+    @pl.loop(0, cells // CHUNK)
+    def _(i):
+        start = pl.multiple_of(i * CHUNK, LANES)
+        wide = psi[:, pl.ds(start, CHUNK + 2 * PAD)]
+
+        def shifted(offset):
+            return wide[:, PAD + offset : PAD + offset + CHUNK]
+
+        here = pot[:, pl.ds(start, CHUNK)] + (-1.5 * STENCIL[0])
+        total = jnp.concatenate([here, here], axis=0) * shifted(0)
+        for k in range(1, 5):
+            total = total + (-0.5 * STENCIL[k]) * (shifted(NY * k) + shifted(-NY * k))
+            up, down = ycoef[k - 1], ycoef[3 + k]
+            total = total + jnp.concatenate([up, up], axis=0) * shifted(k)
+            total = total + jnp.concatenate([down, down], axis=0) * shifted(-k)
+        h[:, pl.ds(start, CHUNK)] = total
+
+    h_copies = spread(h, 0, got_h, h_send, h_recv, 1)
+    keep_own(h, 0, got_h)
+
+    keep_own(psi, PAD, got_psi)
+
     @pl.loop(0, 48)
     def _(i):
         table_copy(i).wait()
@@ -314,8 +345,6 @@
     widen = ones_where((row >> 2) == (col >> 2))
     sums = dot(dot(gather, raw, NN), widen, NN)
     part[...] = sums
-    for copy in small_loads:
-        copy.wait()
     row, col = iota(16, 8)
     kinds = jnp.concatenate(
         [jnp.broadcast_to(energy[0, a : a + 1, :], (8, 8)) for a in range(2)], axis=0
@@ -342,25 +371,6 @@
         copy.start()
         part_copies.append(copy)
 
-    @pl.loop(0, cells // CHUNK)
-    def _(i):
-        start = pl.multiple_of(i * CHUNK, LANES)
-        wide = psi[:, pl.ds(start, CHUNK + 2 * PAD)]
-
-        def shifted(offset):
-            return wide[:, PAD + offset : PAD + offset + CHUNK]
-
-        here = pot[:, pl.ds(start, CHUNK)] + (-1.5 * STENCIL[0])
-        total = jnp.concatenate([here, here], axis=0) * shifted(0)
-        for k in range(1, 5):
-            total = total + (-0.5 * STENCIL[k]) * (shifted(NY * k) + shifted(-NY * k))
-            up, down = ycoef[k - 1], ycoef[3 + k]
-            total = total + jnp.concatenate([up, up], axis=0) * shifted(k)
-            total = total + jnp.concatenate([down, down], axis=0) * shifted(-k)
-        h[:, pl.ds(start, CHUNK)] = total
-
-    keep_own(psi, PAD, got_psi)
-
     for copy in halo:
         copy.wait_recv()
     across = z_matrix()
@@ -372,10 +382,7 @@
         planes = jnp.concatenate(
             [before[:, here], psi[:, pl.ds(start + PAD, WIDE)], after[:, here]], axis=0
         )
-        h[:, here] = h[:, here] + dot(across, planes, NN)
-
-    h_copies = spread(h, 0, got_h, h_send, h_recv, 1)
-    keep_own(h, 0, got_h)
+        full[:, here] = h[:, here] + dot(across, planes, NN)
 
     for copy in part_copies:
         copy.wait_recv()
@@ -411,6 +418,25 @@
     def _():
         owners[me_b] = owner[...]
 
+    await_spread(psi_copies, psi, PAD, got_psi, 0)
+
+    def next_copy(first, width, sem):
+        return pltpu.make_async_remote_copy(
+            src_ref=got_psi.at[:, pl.ds(first, width)],
+            dst_ref=got_next.at[:, pl.ds(first, width)],
+            send_sem=next_send.at[sem],
+            recv_sem=next_recv.at[sem],
+            device_id=(grid_peer(-1), me_b),
+            device_id_type=MESH,
+        )
+
+    holds_extra = (me_b == extras[0][1]) | (me_b == extras[1][1])
+    next_copy(0, share, 0).start()
+
+    @pl.when(holds_extra)
+    def _():
+        next_copy(share, LANES, 1).start()
+
     row, col = iota(48, 192)
     repeat = ones_where(row == (col >> 2))
     spread_coef = dot(coef, repeat, TN)[0:16, :]
@@ -421,7 +447,7 @@
     def _(i):
         start = pl.multiple_of(i * WIDE, LANES)
         here = pl.ds(start, WIDE)
-        full[:, here] = h[:, here] + dot(spread_coef, table[:, here], NN)
+        full[:, here] = full[:, here] + dot(spread_coef, table[:, here], NN)
 
     stores = [
         pltpu.make_async_copy(full.at[pl.ds(4 * b, 4), :], h_out.at[b], out_sem.at[b])
@@ -453,12 +479,32 @@
     narrow = ones_where((row >> 2) == col)
     row, col = iota(rows, rows)
     same_plane = (row & 3) == (col & 3)
-    await_spread(psi_copies, psi, PAD, got_psi, 0)
+    apart = jnp.abs((row & 3) - (col & 3))
+    above = (col & 3) + 4 - (row & 3)
+    below = (row & 3) + 4 - (col & 3)
+
+    def coupled(distance):
+        value = jnp.zeros((rows, rows), jnp.float32)
+        for k in range(1, 5):
+            value = jnp.where(distance == k, -0.5 * STENCIL[k], value)
+        return value
+
     bands = got_psi[...]
-    corr = jnp.where(same_plane, dot(bands, bands, NT), 0.0)
+    pairs = dot(bands, bands, NT)
+    corr = jnp.where(same_plane, pairs, 0.0)
     early = dot(pick_nonlocal, nonlocal_gram, NN) + dot(dot(pick_corr, corr, NN), narrow, NN)
+    across_gram = coupled(apart) * pairs
+    next_copy(0, share, 0).wait_recv()
+
+    @pl.when(holds_extra)
+    def _():
+        next_copy(share, LANES, 1).wait_recv()
+
+    following = got_next[...]
+    across_gram = across_gram + coupled(above) * dot(bands, following, NT)
+    across_gram = across_gram + coupled(below) * dot(following, bands, NT)
     await_spread(h_copies, h, 0, got_h, 1)
-    gram = jnp.where(same_plane, dot(got_h[...], bands, NT), 0.0)
+    gram = jnp.where(same_plane, dot(got_h[...], bands, NT), 0.0) + across_gram
     blocks = early + dot(dot(pick_gram, gram, NN), narrow, NN)
     terms[...] = blocks.reshape(nb, 8, LANES)
 
@@ -523,6 +569,12 @@
     await_sent(psi_copies, psi, PAD, got_psi, 0)
     await_sent(h_copies, h, 0, got_h, 1)
 
+    next_copy(0, share, 0).wait_send()
+
+    @pl.when(holds_extra)
+    def _():
+        next_copy(share, LANES, 1).wait_send()
+
     @pl.when(me_b != root)
     def _():
         owner_copy(me_b).wait_send()
@@ -531,17 +583,23 @@
         copy.wait()
 
 
-def finish(h_in, sums_in, h_out, corr_out, gram_out, held, sem):
+def finish(h_in, sums_in, h_out, corr_out, gram_out, held, sums, corr, gram, sem):
     ins = [pltpu.make_async_copy(h_in.at[b], held.at[b], sem.at[b]) for b in range(4)]
     outs = [pltpu.make_async_copy(held.at[b], h_out.at[b], sem.at[4 + b]) for b in range(4)]
+    sums_copy = pltpu.make_async_copy(sums_in, sums, sem.at[8])
+    outs.append(pltpu.make_async_copy(corr, corr_out, sem.at[9]))
+    outs.append(pltpu.make_async_copy(gram, gram_out, sem.at[10]))
+    sums_copy.start()
     for copy in ins:
         copy.start()
     width = corr_out.shape[1]
-    corr_out[...] = sums_in[0:4, 0:width]
-    gram_out[...] = sums_in[4:8, 0:width]
-    for copy, onward in zip(ins, outs):
+    sums_copy.wait()
+    corr[...] = sums[0:4, 0:width]
+    gram[...] = sums[4:8, 0:width]
+    for copy in ins:
         copy.wait()
-        onward.start()
+    for copy in outs:
+        copy.start()
     for copy in outs:
         copy.wait()
 
@@ -576,6 +634,7 @@
             pltpu.VMEM((16, cells), f32),
             pltpu.VMEM((16 * nb, width), f32),
             pltpu.VMEM((16 * nb, width), f32),
+            pltpu.VMEM((16 * nb, width), f32),
             pltpu.VMEM((8, 8, CHUNK), f32),
             pltpu.VMEM((64, LANES), f32),
             pltpu.VMEM((48, LANES), f32),
@@ -602,6 +661,8 @@
             dma((nb,)),
             dma((4,)),
             dma((32,)),
+            dma((2,)),
+            dma((2,)),
             dma,
             dma((nb,)),
             dma((4,)),
@@ -632,9 +693,15 @@
             jax.ShapeDtypeStruct((groups, groups * nb), f32),
             jax.ShapeDtypeStruct((groups, groups * nb), f32),
         ),
-        in_specs=[any_space, vmem],
-        out_specs=(any_space, vmem, vmem),
-        scratch_shapes=[pltpu.VMEM(orbitals.shape, f32), dma((8,))],
+        in_specs=[any_space, any_space],
+        out_specs=(any_space, any_space, any_space),
+        scratch_shapes=[
+            pltpu.VMEM(orbitals.shape, f32),
+            pltpu.VMEM((8, LANES), f32),
+            pltpu.VMEM((groups, groups * nb), f32),
+            pltpu.VMEM((groups, groups * nb), f32),
+            dma((11,)),
+        ],
         compiler_params=pltpu.CompilerParams(vmem_limit_bytes=60 * 2**20),
         cost_estimate=pl.CostEstimate(flops=0, bytes_accessed=900_000, transcendentals=0),
     )(full, sums)

time: 81.2 us -> 81.6 us (level)
    pallas_call x1, Pallas kernels: 77.3 us -> 78.9 us  [shards(): pl.pallas_call(functools.partial(kernel, dims), out_shape=(jax.ShapeDtype...]
    pallas_call x1, Pallas kernels: 3.02 us -> 1.89 us  [shards(): pl.pallas_call(finish, out_shape=(jax.ShapeDtypeStruct(orbitals.shape, f3...]
where the time goes in v4:
time: 81.6 us; the launch traced here: 81.5 us
  Pallas kernels  80.8 us (99%)
    pallas_call x1, Pallas kernels, shards(): pl.pallas_call(functools.partial(kernel, dims), out_shape=(jax.ShapeDtype...  78.9 us
    pallas_call x1, Pallas kernels, shards(): pl.pallas_call(finish, out_shape=(jax.ShapeDtypeStruct(orbitals.shape, f3...  1.89 us

profile of v4, /device:TPU:1, one launch (start us, length us, event | category | flops | bytes accessed | tf_op | source)
XLA Modules:
  0.0 81.5 jit_solution(2025167513536725010)
XLA Ops:
  0.6 78.9 %shard_map.76 = (f32[4,4,6400]{2,1,0:T(4,128)}, f32[8,128]{1,0:T(8,128)}) custom-call(f32[4,4,6400]{2,1,0:T(4,128)} %psi_in.1, f32[4,6400]{1,0:T(4,128)} %pot_in.1, f32[48,4,6400]{2,1,0:T(4,128)} %bitcast.1, f32[1,2,8]{2,1,0:T(2,128)} %energy_in.1, s32[1,2]{1,0:T(1,128)} %count_in.1), custom_call_target="tpu_custom_call" | custom-call | flops 80000000 | bytes 6000000 | tf_op jit(solution)/shard_map/pallas_call | solution.py:617
  79.6 1.9 %shard_map.77 = (f32[4,4,6400]{2,1,0:T(4,128)}, f32[4,64]{1,0:T(4,128)}, f32[4,64]{1,0:T(4,128)}) custom-call(f32[4,4,6400]{2,1,0:T(4,128)} %get-tuple-element.5.h_in, f32[8,128]{1,0:T(8,128)} %get-tuple-element.6.sums_in), custom_call_target="tpu_custom_call" | custom-call | bytes 900000 | tf_op jit(solution)/shard_map/pallas_call | solution.py:689

commit v5 on v4

--- a/solution.py
+++ b/solution.py
@@ -287,19 +287,6 @@
 
     psi_copies = spread(psi, PAD, got_psi, psi_send, psi_recv, 0)
 
-    halo = []
-    for i, (step, target) in enumerate(((1, before), (-1, after))):
-        copy = pltpu.make_async_remote_copy(
-            src_ref=psi.at[:, pl.ds(PAD, cells)],
-            dst_ref=target,
-            send_sem=halo_send.at[i],
-            recv_sem=halo_recv.at[i],
-            device_id=(grid_peer(step), me_b),
-            device_id_type=MESH,
-        )
-        copy.start()
-        halo.append(copy)
-
     for copy in small_loads:
         copy.wait()
 
@@ -371,18 +358,24 @@
         copy.start()
         part_copies.append(copy)
 
-    for copy in halo:
-        copy.wait_recv()
-    across = z_matrix()
-
-    @pl.loop(0, cells // WIDE)
-    def _(i):
-        start = pl.multiple_of(i * WIDE, LANES)
-        here = pl.ds(start, WIDE)
-        planes = jnp.concatenate(
-            [before[:, here], psi[:, pl.ds(start + PAD, WIDE)], after[:, here]], axis=0
-        )
-        full[:, here] = h[:, here] + dot(across, planes, NN)
+    await_spread(psi_copies, psi, PAD, got_psi, 0)
+
+    def next_copy(first, width, sem):
+        return pltpu.make_async_remote_copy(
+            src_ref=got_psi.at[:, pl.ds(first, width)],
+            dst_ref=got_next.at[:, pl.ds(first, width)],
+            send_sem=next_send.at[sem],
+            recv_sem=next_recv.at[sem],
+            device_id=(grid_peer(-1), me_b),
+            device_id_type=MESH,
+        )
+
+    holds_extra = (me_b == extras[0][1]) | (me_b == extras[1][1])
+    next_copy(0, share, 0).start()
+
+    @pl.when(holds_extra)
+    def _():
+        next_copy(share, LANES, 1).start()
 
     for copy in part_copies:
         copy.wait_recv()
@@ -418,54 +411,24 @@
     def _():
         owners[me_b] = owner[...]
 
-    await_spread(psi_copies, psi, PAD, got_psi, 0)
-
-    def next_copy(first, width, sem):
-        return pltpu.make_async_remote_copy(
-            src_ref=got_psi.at[:, pl.ds(first, width)],
-            dst_ref=got_next.at[:, pl.ds(first, width)],
-            send_sem=next_send.at[sem],
-            recv_sem=next_recv.at[sem],
-            device_id=(grid_peer(-1), me_b),
-            device_id_type=MESH,
-        )
-
-    holds_extra = (me_b == extras[0][1]) | (me_b == extras[1][1])
-    next_copy(0, share, 0).start()
-
-    @pl.when(holds_extra)
-    def _():
-        next_copy(share, LANES, 1).start()
-
     row, col = iota(48, 192)
     repeat = ones_where(row == (col >> 2))
     spread_coef = dot(coef, repeat, TN)[0:16, :]
     row, col = iota(16, 192)
     spread_coef = jnp.where((row & 3) == (col & 3), spread_coef, 0.0)
 
-    @pl.loop(0, cells // WIDE)
-    def _(i):
-        start = pl.multiple_of(i * WIDE, LANES)
-        here = pl.ds(start, WIDE)
-        full[:, here] = full[:, here] + dot(spread_coef, table[:, here], NN)
-
-    stores = [
-        pltpu.make_async_copy(full.at[pl.ds(4 * b, 4), :], h_out.at[b], out_sem.at[b])
-        for b in range(4)
-    ]
-    for copy in stores:
+    halo = []
+    for i, (step, target) in enumerate(((1, before), (-1, after))):
+        copy = pltpu.make_async_remote_copy(
+            src_ref=psi.at[:, pl.ds(PAD, cells)],
+            dst_ref=target,
+            send_sem=halo_send.at[i],
+            recv_sem=halo_recv.at[i],
+            device_id=(grid_peer(step), me_b),
+            device_id_type=MESH,
+        )
         copy.start()
-
-    @pl.when(me_b == root)
-    def _():
-        for other in range(nb):
-
-            @pl.when(other != me_b)
-            def _(other=other):
-                owner_copy(other).wait_recv()
-
-    projections = jnp.sum(owners[...], axis=0)
-    nonlocal_gram = dot(projections * weight, projections, TN)
+        halo.append(copy)
 
     rows = 16 * nb
     row, col = iota(8 * nb, rows)
@@ -492,20 +455,32 @@
     bands = got_psi[...]
     pairs = dot(bands, bands, NT)
     corr = jnp.where(same_plane, pairs, 0.0)
-    early = dot(pick_nonlocal, nonlocal_gram, NN) + dot(dot(pick_corr, corr, NN), narrow, NN)
+    early = dot(dot(pick_corr, corr, NN), narrow, NN)
     across_gram = coupled(apart) * pairs
-    next_copy(0, share, 0).wait_recv()
-
-    @pl.when(holds_extra)
-    def _():
-        next_copy(share, LANES, 1).wait_recv()
-
-    following = got_next[...]
-    across_gram = across_gram + coupled(above) * dot(bands, following, NT)
-    across_gram = across_gram + coupled(below) * dot(following, bands, NT)
     await_spread(h_copies, h, 0, got_h, 1)
     gram = jnp.where(same_plane, dot(got_h[...], bands, NT), 0.0) + across_gram
-    blocks = early + dot(dot(pick_gram, gram, NN), narrow, NN)
+    next_copy(0, share, 0).wait_recv()
+
+    @pl.when(holds_extra)
+    def _():
+        next_copy(share, LANES, 1).wait_recv()
+
+    following = got_next[...]
+    gram = gram + coupled(above) * dot(bands, following, NT)
+    gram = gram + coupled(below) * dot(following, bands, NT)
+    @pl.when(me_b == root)
+    def _():
+        for other in range(nb):
+
+            @pl.when(other != me_b)
+            def _(other=other):
+                owner_copy(other).wait_recv()
+
+    projections = jnp.sum(owners[...], axis=0)
+    nonlocal_gram = dot(projections * weight, projections, TN)
+
+    blocks = early + dot(pick_nonlocal, nonlocal_gram, NN)
+    blocks = blocks + dot(dot(pick_gram, gram, NN), narrow, NN)
     terms[...] = blocks.reshape(nb, 8, LANES)
 
     def exchange(source_of, target, slot, peers_, send, recv):
@@ -546,6 +521,20 @@
         y_recv,
     )
     y_terms[slot] = x_sum[my_h]
+
+    for copy in halo:
+        copy.wait_recv()
+    across = z_matrix()
+
+    @pl.loop(0, cells // WIDE)
+    def _(i):
+        start = pl.multiple_of(i * WIDE, LANES)
+        here = pl.ds(start, WIDE)
+        planes = jnp.concatenate(
+            [before[:, here], psi[:, pl.ds(start + PAD, WIDE)], after[:, here]], axis=0
+        )
+        full[:, here] = h[:, here] + dot(across, planes, NN)
+
     for copy in y_copies:
         copy.wait_recv()
     y_sum[...] = jnp.sum(y_terms[...], axis=0)
@@ -560,6 +549,20 @@
         z_recv,
     )
     z_terms[slot] = y_sum[...]
+
+    @pl.loop(0, cells // WIDE)
+    def _(i):
+        start = pl.multiple_of(i * WIDE, LANES)
+        here = pl.ds(start, WIDE)
+        full[:, here] = full[:, here] + dot(spread_coef, table[:, here], NN)
+
+    stores = [
+        pltpu.make_async_copy(full.at[pl.ds(4 * b, 4), :], h_out.at[b], out_sem.at[b])
+        for b in range(4)
+    ]
+    for copy in stores:
+        copy.start()
+
     for copy in z_copies:
         copy.wait_recv()
     sums_out[...] = jnp.sum(z_terms[...], axis=0) * (1.0 / (4 * cells * ng))

time: 81.6 us -> 75.5 us (0.925)
  Pallas kernels: 80.8 us -> 74.7 us
    pallas_call x1, Pallas kernels: 78.9 us -> 72.8 us  [shards(): pl.pallas_call(functools.partial(kernel, dims), out_shape=(jax.ShapeDtype...]
where the time goes in v5:
time: 75.5 us; the launch traced here: 75.3 us
  Pallas kernels  74.7 us (99%)
    pallas_call x1, Pallas kernels, shards(): pl.pallas_call(functools.partial(kernel, dims), out_shape=(jax.ShapeDtype...  72.8 us
    pallas_call x1, Pallas kernels, shards(): pl.pallas_call(finish, out_shape=(jax.ShapeDtypeStruct(orbitals.shape, f3...  1.89 us

profile of v5, /device:TPU:1, one launch (start us, length us, event | category | flops | bytes accessed | tf_op | source)
XLA Modules:
  0.0 75.3 jit_solution(11134511268344148194)
XLA Ops:
  0.6 72.8 %shard_map.76 = (f32[4,4,6400]{2,1,0:T(4,128)}, f32[8,128]{1,0:T(8,128)}) custom-call(f32[4,4,6400]{2,1,0:T(4,128)} %psi_in.1, f32[4,6400]{1,0:T(4,128)} %pot_in.1, f32[48,4,6400]{2,1,0:T(4,128)} %bitcast.1, f32[1,2,8]{2,1,0:T(2,128)} %energy_in.1, s32[1,2]{1,0:T(1,128)} %count_in.1), custom_call_target="tpu_custom_call" | custom-call | flops 80000000 | bytes 6000000 | tf_op jit(solution)/shard_map/pallas_call | solution.py:620
  73.4 1.9 %shard_map.77 = (f32[4,4,6400]{2,1,0:T(4,128)}, f32[4,64]{1,0:T(4,128)}, f32[4,64]{1,0:T(4,128)}) custom-call(f32[4,4,6400]{2,1,0:T(4,128)} %get-tuple-element.5.h_in, f32[8,128]{1,0:T(8,128)} %get-tuple-element.6.sums_in), custom_call_target="tpu_custom_call" | custom-call | bytes 900000 | tf_op jit(solution)/shard_map/pallas_call | solution.py:692

commit v6 on v5

--- a/solution.py
+++ b/solution.py
@@ -122,7 +122,10 @@
     my_x, my_h = me_b // 2, me_b % 2
     my_c, my_z, my_y = me_g % 2, (me_g // 2) % nz, me_g // (2 * nz)
 
-    extras = [(per * nb + i, (0, nx + 1)[i]) for i in range(cells // LANES - per * nb)]
+    def extra_owner(i, core):
+        return ((i * (nx // 2) + core * max(nx // 4, 1)) % nx) * 2 + i
+
+    extras = [(per * nb + i, extra_owner(i, my_c)) for i in range(cells // LANES - per * nb)]
     far_x = sorted(range(nx), key=lambda dx: -min(dx, nx - dx))
     far_z = sorted(range(nz), key=lambda dz: -min(dz, nz - dz))
     band_offsets = [(dx, dh) for dh in (1, 0) for dx in far_x if (dx, dh) != (0, 0)]
@@ -161,6 +164,15 @@
     ]:
         pl.semaphore_signal(barrier, inc=1, device_id=peer, device_id_type=MESH)
         peers += 1
+
+    other_x = (my_x + max(nx // 4, 1) * (1 - 2 * my_c) + nx) % nx
+    pl.semaphore_signal(
+        barrier,
+        inc=1,
+        device_id=(grid_peer(1), other_x * 2 + my_h),
+        device_id_type=MESH,
+    )
+    peers += 1
 
     loads = [
         pltpu.make_async_copy(
@@ -271,7 +283,9 @@
             @pl.when(me_b == owner)
             def _(i=i, tile=tile, owner=owner):
                 for other in range(nb):
-                    if other != owner:
+
+                    @pl.when(other != owner)
+                    def _(other=other):
                         extra_copy(
                             source, base, target, which, i, tile, owner, other
                         ).wait_recv()
@@ -289,28 +303,6 @@
 
     for copy in small_loads:
         copy.wait()
-
-    @pl.loop(0, cells // CHUNK)
-    def _(i):
-        start = pl.multiple_of(i * CHUNK, LANES)
-        wide = psi[:, pl.ds(start, CHUNK + 2 * PAD)]
-
-        def shifted(offset):
-            return wide[:, PAD + offset : PAD + offset + CHUNK]
-
-        here = pot[:, pl.ds(start, CHUNK)] + (-1.5 * STENCIL[0])
-        total = jnp.concatenate([here, here], axis=0) * shifted(0)
-        for k in range(1, 5):
-            total = total + (-0.5 * STENCIL[k]) * (shifted(NY * k) + shifted(-NY * k))
-            up, down = ycoef[k - 1], ycoef[3 + k]
-            total = total + jnp.concatenate([up, up], axis=0) * shifted(k)
-            total = total + jnp.concatenate([down, down], axis=0) * shifted(-k)
-        h[:, pl.ds(start, CHUNK)] = total
-
-    h_copies = spread(h, 0, got_h, h_send, h_recv, 1)
-    keep_own(h, 0, got_h)
-
-    keep_own(psi, PAD, got_psi)
 
     @pl.loop(0, 48)
     def _(i):
@@ -358,24 +350,49 @@
         copy.start()
         part_copies.append(copy)
 
+    @pl.loop(0, cells // CHUNK)
+    def _(i):
+        start = pl.multiple_of(i * CHUNK, LANES)
+        wide = psi[:, pl.ds(start, CHUNK + 2 * PAD)]
+
+        def shifted(offset):
+            return wide[:, PAD + offset : PAD + offset + CHUNK]
+
+        here = pot[:, pl.ds(start, CHUNK)] + (-1.5 * STENCIL[0])
+        total = jnp.concatenate([here, here], axis=0) * shifted(0)
+        for k in range(1, 5):
+            total = total + (-0.5 * STENCIL[k]) * (shifted(NY * k) + shifted(-NY * k))
+            up, down = ycoef[k - 1], ycoef[3 + k]
+            total = total + jnp.concatenate([up, up], axis=0) * shifted(k)
+            total = total + jnp.concatenate([down, down], axis=0) * shifted(-k)
+        h[:, pl.ds(start, CHUNK)] = total
+
+    h_copies = spread(h, 0, got_h, h_send, h_recv, 1)
+    keep_own(h, 0, got_h)
+
+    keep_own(psi, PAD, got_psi)
+
     await_spread(psi_copies, psi, PAD, got_psi, 0)
 
-    def next_copy(first, width, sem):
+    def next_copy(first, width, sem, target):
         return pltpu.make_async_remote_copy(
             src_ref=got_psi.at[:, pl.ds(first, width)],
             dst_ref=got_next.at[:, pl.ds(first, width)],
             send_sem=next_send.at[sem],
             recv_sem=next_recv.at[sem],
-            device_id=(grid_peer(-1), me_b),
+            device_id=(grid_peer(-1), target),
             device_id_type=MESH,
         )
 
-    holds_extra = (me_b == extras[0][1]) | (me_b == extras[1][1])
-    next_copy(0, share, 0).start()
-
-    @pl.when(holds_extra)
-    def _():
-        next_copy(share, LANES, 1).start()
+    def each_extra(act):
+        for _, owner in extras:
+
+            @pl.when(me_b == owner)
+            def _():
+                act(next_copy(share, LANES, 1, other_x * 2 + my_h))
+
+    next_copy(0, share, 0, me_b).start()
+    each_extra(lambda copy: copy.start())
 
     for copy in part_copies:
         copy.wait_recv()
@@ -416,19 +433,6 @@
     spread_coef = dot(coef, repeat, TN)[0:16, :]
     row, col = iota(16, 192)
     spread_coef = jnp.where((row & 3) == (col & 3), spread_coef, 0.0)
-
-    halo = []
-    for i, (step, target) in enumerate(((1, before), (-1, after))):
-        copy = pltpu.make_async_remote_copy(
-            src_ref=psi.at[:, pl.ds(PAD, cells)],
-            dst_ref=target,
-            send_sem=halo_send.at[i],
-            recv_sem=halo_recv.at[i],
-            device_id=(grid_peer(step), me_b),
-            device_id_type=MESH,
-        )
-        copy.start()
-        halo.append(copy)
 
     rows = 16 * nb
     row, col = iota(8 * nb, rows)
@@ -444,7 +448,6 @@
     same_plane = (row & 3) == (col & 3)
     apart = jnp.abs((row & 3) - (col & 3))
     above = (col & 3) + 4 - (row & 3)
-    below = (row & 3) + 4 - (col & 3)
 
     def coupled(distance):
         value = jnp.zeros((rows, rows), jnp.float32)
@@ -459,15 +462,25 @@
     across_gram = coupled(apart) * pairs
     await_spread(h_copies, h, 0, got_h, 1)
     gram = jnp.where(same_plane, dot(got_h[...], bands, NT), 0.0) + across_gram
-    next_copy(0, share, 0).wait_recv()
-
-    @pl.when(holds_extra)
-    def _():
-        next_copy(share, LANES, 1).wait_recv()
+    halo = []
+    for i, (step, target) in enumerate(((1, before), (-1, after))):
+        copy = pltpu.make_async_remote_copy(
+            src_ref=psi.at[:, pl.ds(PAD, cells)],
+            dst_ref=target,
+            send_sem=halo_send.at[i],
+            recv_sem=halo_recv.at[i],
+            device_id=(grid_peer(step), me_b),
+            device_id_type=MESH,
+        )
+        copy.start()
+        halo.append(copy)
+
+    next_copy(0, share, 0, me_b).wait_recv()
+    each_extra(lambda copy: copy.wait_recv())
 
     following = got_next[...]
-    gram = gram + coupled(above) * dot(bands, following, NT)
-    gram = gram + coupled(below) * dot(following, bands, NT)
+    crossing = dot(coupled(above) * dot(bands, following, NT), narrow, NN)
+    crossing = dot(narrow, crossing, TN)
     @pl.when(me_b == root)
     def _():
         for other in range(nb):
@@ -479,7 +492,8 @@
     projections = jnp.sum(owners[...], axis=0)
     nonlocal_gram = dot(projections * weight, projections, TN)
 
-    blocks = early + dot(pick_nonlocal, nonlocal_gram, NN)
+    blocks = early + dot(pick_nonlocal, nonlocal_gram + crossing, NN)
+    blocks = blocks + dot(pick_nonlocal, crossing, NT)
     blocks = blocks + dot(dot(pick_gram, gram, NN), narrow, NN)
     terms[...] = blocks.reshape(nb, 8, LANES)
 
@@ -572,11 +586,8 @@
     await_sent(psi_copies, psi, PAD, got_psi, 0)
     await_sent(h_copies, h, 0, got_h, 1)
 
-    next_copy(0, share, 0).wait_send()
-
-    @pl.when(holds_extra)
-    def _():
-        next_copy(share, LANES, 1).wait_send()
+    next_copy(0, share, 0, me_b).wait_send()
+    each_extra(lambda copy: copy.wait_send())
 
     @pl.when(me_b != root)
     def _():

time: 75.5 us -> 72.5 us (0.960)
  Pallas kernels: 74.7 us -> 71.7 us
    pallas_call x1, Pallas kernels: 72.8 us -> 69.8 us  [shards(): pl.pallas_call(functools.partial(kernel, dims), out_shape=(jax.ShapeDtype...]
where the time goes in v6:
time: 72.5 us; the launch traced here: 72.3 us
  Pallas kernels  71.7 us (99%)
    pallas_call x1, Pallas kernels, shards(): pl.pallas_call(functools.partial(kernel, dims), out_shape=(jax.ShapeDtype...  69.8 us
    pallas_call x1, Pallas kernels, shards(): pl.pallas_call(finish, out_shape=(jax.ShapeDtypeStruct(orbitals.shape, f3...  1.89 us

profile of v6, /device:TPU:1, one launch (start us, length us, event | category | flops | bytes accessed | tf_op | source)
XLA Modules:
  0.0 72.3 jit_solution(6177986970030118885)
XLA Ops:
  0.6 69.8 %shard_map.76 = (f32[4,4,6400]{2,1,0:T(4,128)}, f32[8,128]{1,0:T(8,128)}) custom-call(f32[4,4,6400]{2,1,0:T(4,128)} %psi_in.1, f32[4,6400]{1,0:T(4,128)} %pot_in.1, f32[48,4,6400]{2,1,0:T(4,128)} %bitcast.1, f32[1,2,8]{2,1,0:T(2,128)} %energy_in.1, s32[1,2]{1,0:T(1,128)} %count_in.1), custom_call_target="tpu_custom_call" | custom-call | flops 80000000 | bytes 6000000 | tf_op jit(solution)/shard_map/pallas_call | solution.py:631
  70.4 1.9 %shard_map.77 = (f32[4,4,6400]{2,1,0:T(4,128)}, f32[4,64]{1,0:T(4,128)}, f32[4,64]{1,0:T(4,128)}) custom-call(f32[4,4,6400]{2,1,0:T(4,128)} %get-tuple-element.5.h_in, f32[8,128]{1,0:T(8,128)} %get-tuple-element.6.sums_in), custom_call_target="tpu_custom_call" | custom-call | bytes 900000 | tf_op jit(solution)/shard_map/pallas_call | solution.py:703

commit v7 on v6

--- a/solution.py
+++ b/solution.py
@@ -147,6 +147,15 @@
     def grid_peer(step):
         return (me_g + step + ng) % ng
 
+    loads = [
+        pltpu.make_async_copy(
+            psi_in.at[b], psi.at[pl.ds(4 * b, 4), pl.ds(PAD, cells)], in_sem.at[b]
+        )
+        for b in range(4)
+    ]
+    for copy in loads:
+        copy.start()
+
     barrier = pltpu.get_barrier_semaphore()
     peers = 0
     for dx, dh in band_offsets:
@@ -174,18 +183,10 @@
     )
     peers += 1
 
-    loads = [
-        pltpu.make_async_copy(
-            psi_in.at[b], psi.at[pl.ds(4 * b, 4), pl.ds(PAD, cells)], in_sem.at[b]
-        )
-        for b in range(4)
-    ]
     pot_loads = [
         pltpu.make_async_copy(pot_in, pot.at[pl.ds(4 * b, 4), :], in_sem.at[4 + b])
         for b in range(2)
     ]
-    for copy in loads:
-        copy.start()
     small_loads = pot_loads + [
         pltpu.make_async_copy(energy_in, energy, in_sem.at[6]),
         pltpu.make_async_copy(count_in, count, in_sem.at[7]),
@@ -372,28 +373,6 @@
 
     keep_own(psi, PAD, got_psi)
 
-    await_spread(psi_copies, psi, PAD, got_psi, 0)
-
-    def next_copy(first, width, sem, target):
-        return pltpu.make_async_remote_copy(
-            src_ref=got_psi.at[:, pl.ds(first, width)],
-            dst_ref=got_next.at[:, pl.ds(first, width)],
-            send_sem=next_send.at[sem],
-            recv_sem=next_recv.at[sem],
-            device_id=(grid_peer(-1), target),
-            device_id_type=MESH,
-        )
-
-    def each_extra(act):
-        for _, owner in extras:
-
-            @pl.when(me_b == owner)
-            def _():
-                act(next_copy(share, LANES, 1, other_x * 2 + my_h))
-
-    next_copy(0, share, 0, me_b).start()
-    each_extra(lambda copy: copy.start())
-
     for copy in part_copies:
         copy.wait_recv()
     total = part[16:32, :] + high1[0:16, :] + low1[32:48, :]
@@ -427,6 +406,28 @@
     @pl.when(me_b == root)
     def _():
         owners[me_b] = owner[...]
+
+    await_spread(psi_copies, psi, PAD, got_psi, 0)
+
+    def next_copy(first, width, sem, target):
+        return pltpu.make_async_remote_copy(
+            src_ref=got_psi.at[:, pl.ds(first, width)],
+            dst_ref=got_next.at[:, pl.ds(first, width)],
+            send_sem=next_send.at[sem],
+            recv_sem=next_recv.at[sem],
+            device_id=(grid_peer(-1), target),
+            device_id_type=MESH,
+        )
+
+    def each_extra(act):
+        for _, owner in extras:
+
+            @pl.when(me_b == owner)
+            def _():
+                act(next_copy(share, LANES, 1, other_x * 2 + my_h))
+
+    next_copy(0, share, 0, me_b).start()
+    each_extra(lambda copy: copy.start())
 
     row, col = iota(48, 192)
     repeat = ones_where(row == (col >> 2))
@@ -462,6 +463,7 @@
     across_gram = coupled(apart) * pairs
     await_spread(h_copies, h, 0, got_h, 1)
     gram = jnp.where(same_plane, dot(got_h[...], bands, NT), 0.0) + across_gram
+    early = early + dot(dot(pick_gram, gram, NN), narrow, NN)
     halo = []
     for i, (step, target) in enumerate(((1, before), (-1, after))):
         copy = pltpu.make_async_remote_copy(
@@ -494,7 +496,6 @@
 
     blocks = early + dot(pick_nonlocal, nonlocal_gram + crossing, NN)
     blocks = blocks + dot(pick_nonlocal, crossing, NT)
-    blocks = blocks + dot(dot(pick_gram, gram, NN), narrow, NN)
     terms[...] = blocks.reshape(nb, 8, LANES)
 
     def exchange(source_of, target, slot, peers_, send, recv):
@@ -536,19 +537,6 @@
     )
     y_terms[slot] = x_sum[my_h]
 
-    for copy in halo:
-        copy.wait_recv()
-    across = z_matrix()
-
-    @pl.loop(0, cells // WIDE)
-    def _(i):
-        start = pl.multiple_of(i * WIDE, LANES)
-        here = pl.ds(start, WIDE)
-        planes = jnp.concatenate(
-            [before[:, here], psi[:, pl.ds(start + PAD, WIDE)], after[:, here]], axis=0
-        )
-        full[:, here] = h[:, here] + dot(across, planes, NN)
-
     for copy in y_copies:
         copy.wait_recv()
     y_sum[...] = jnp.sum(y_terms[...], axis=0)
@@ -564,11 +552,19 @@
     )
     z_terms[slot] = y_sum[...]
 
+    for copy in halo:
+        copy.wait_recv()
+    left = jnp.concatenate([spread_coef, z_matrix()], axis=1)
+
     @pl.loop(0, cells // WIDE)
     def _(i):
         start = pl.multiple_of(i * WIDE, LANES)
         here = pl.ds(start, WIDE)
-        full[:, here] = full[:, here] + dot(spread_coef, table[:, here], NN)
+        right = jnp.concatenate(
+            [table[:, here], before[:, here], psi[:, pl.ds(start + PAD, WIDE)], after[:, here]],
+            axis=0,
+        )
+        full[:, here] = h[:, here] + dot(left, right, NN)
 
     stores = [
         pltpu.make_async_copy(full.at[pl.ds(4 * b, 4), :], h_out.at[b], out_sem.at[b])

time: 72.5 us -> 73.6 us (1.015)
  Pallas kernels: 71.7 us -> 72.8 us
    pallas_call x1, Pallas kernels: 69.8 us -> 70.9 us  [shards(): pl.pallas_call(functools.partial(kernel, dims), out_shape=(jax.ShapeDtype...]
where the time goes in v7:
time: 73.6 us; the launch traced here: 73.4 us
  Pallas kernels  72.8 us (99%)
    pallas_call x1, Pallas kernels, shards(): pl.pallas_call(functools.partial(kernel, dims), out_shape=(jax.ShapeDtype...  70.9 us
    pallas_call x1, Pallas kernels, shards(): pl.pallas_call(finish, out_shape=(jax.ShapeDtypeStruct(orbitals.shape, f3...  1.89 us

profile of v7, /device:TPU:1, one launch (start us, length us, event | category | flops | bytes accessed | tf_op | source)
XLA Modules:
  0.0 73.4 jit_solution(12174855150440310292)
XLA Ops:
  0.6 70.9 %shard_map.76 = (f32[4,4,6400]{2,1,0:T(4,128)}, f32[8,128]{1,0:T(8,128)}) custom-call(f32[4,4,6400]{2,1,0:T(4,128)} %psi_in.1, f32[4,6400]{1,0:T(4,128)} %pot_in.1, f32[48,4,6400]{2,1,0:T(4,128)} %bitcast.1, f32[1,2,8]{2,1,0:T(2,128)} %energy_in.1, s32[1,2]{1,0:T(1,128)} %count_in.1), custom_call_target="tpu_custom_call" | custom-call | flops 80000000 | bytes 6000000 | tf_op jit(solution)/shard_map/pallas_call | solution.py:627
  71.6 1.9 %shard_map.77 = (f32[4,4,6400]{2,1,0:T(4,128)}, f32[4,64]{1,0:T(4,128)}, f32[4,64]{1,0:T(4,128)}) custom-call(f32[4,4,6400]{2,1,0:T(4,128)} %get-tuple-element.5.h_in, f32[8,128]{1,0:T(8,128)} %get-tuple-element.6.sums_in), custom_call_target="tpu_custom_call" | custom-call | bytes 900000 | tf_op jit(solution)/shard_map/pallas_call | solution.py:699

commit v8 on v6

--- a/solution.py
+++ b/solution.py
@@ -147,6 +147,15 @@
     def grid_peer(step):
         return (me_g + step + ng) % ng
 
+    loads = [
+        pltpu.make_async_copy(
+            psi_in.at[b], psi.at[pl.ds(4 * b, 4), pl.ds(PAD, cells)], in_sem.at[b]
+        )
+        for b in range(4)
+    ]
+    for copy in loads:
+        copy.start()
+
     barrier = pltpu.get_barrier_semaphore()
     peers = 0
     for dx, dh in band_offsets:
@@ -174,18 +183,10 @@
     )
     peers += 1
 
-    loads = [
-        pltpu.make_async_copy(
-            psi_in.at[b], psi.at[pl.ds(4 * b, 4), pl.ds(PAD, cells)], in_sem.at[b]
-        )
-        for b in range(4)
-    ]
     pot_loads = [
         pltpu.make_async_copy(pot_in, pot.at[pl.ds(4 * b, 4), :], in_sem.at[4 + b])
         for b in range(2)
     ]
-    for copy in loads:
-        copy.start()
     small_loads = pot_loads + [
         pltpu.make_async_copy(energy_in, energy, in_sem.at[6]),
         pltpu.make_async_copy(count_in, count, in_sem.at[7]),
@@ -394,6 +395,19 @@
     next_copy(0, share, 0, me_b).start()
     each_extra(lambda copy: copy.start())
 
+    halo = []
+    for i, (step, target) in enumerate(((1, before), (-1, after))):
+        copy = pltpu.make_async_remote_copy(
+            src_ref=psi.at[:, pl.ds(PAD, cells)],
+            dst_ref=target,
+            send_sem=halo_send.at[i],
+            recv_sem=halo_recv.at[i],
+            device_id=(grid_peer(step), me_b),
+            device_id_type=MESH,
+        )
+        halo.append(copy)
+    halo[0].start()
+
     for copy in part_copies:
         copy.wait_recv()
     total = part[16:32, :] + high1[0:16, :] + low1[32:48, :]
@@ -462,19 +476,8 @@
     across_gram = coupled(apart) * pairs
     await_spread(h_copies, h, 0, got_h, 1)
     gram = jnp.where(same_plane, dot(got_h[...], bands, NT), 0.0) + across_gram
-    halo = []
-    for i, (step, target) in enumerate(((1, before), (-1, after))):
-        copy = pltpu.make_async_remote_copy(
-            src_ref=psi.at[:, pl.ds(PAD, cells)],
-            dst_ref=target,
-            send_sem=halo_send.at[i],
-            recv_sem=halo_recv.at[i],
-            device_id=(grid_peer(step), me_b),
-            device_id_type=MESH,
-        )
-        copy.start()
-        halo.append(copy)
-
+    early = early + dot(dot(pick_gram, gram, NN), narrow, NN)
+    halo[1].start()
     next_copy(0, share, 0, me_b).wait_recv()
     each_extra(lambda copy: copy.wait_recv())
 
@@ -494,7 +497,6 @@
 
     blocks = early + dot(pick_nonlocal, nonlocal_gram + crossing, NN)
     blocks = blocks + dot(pick_nonlocal, crossing, NT)
-    blocks = blocks + dot(dot(pick_gram, gram, NN), narrow, NN)
     terms[...] = blocks.reshape(nb, 8, LANES)
 
     def exchange(source_of, target, slot, peers_, send, recv):

time: 72.5 us -> 74.9 us (1.033)
  Pallas kernels: 71.7 us -> 74.1 us
    pallas_call x1, Pallas kernels: 69.8 us -> 72.2 us  [shards(): pl.pallas_call(functools.partial(kernel, dims), out_shape=(jax.ShapeDtype...]
where the time goes in v8:
time: 74.9 us; the launch traced here: 74.7 us
  Pallas kernels  74.1 us (99%)
    pallas_call x1, Pallas kernels, shards(): pl.pallas_call(functools.partial(kernel, dims), out_shape=(jax.ShapeDtype...  72.2 us
    pallas_call x1, Pallas kernels, shards(): pl.pallas_call(finish, out_shape=(jax.ShapeDtypeStruct(orbitals.shape, f3...  1.89 us

profile of v8, /device:TPU:1, one launch (start us, length us, event | category | flops | bytes accessed | tf_op | source)
XLA Modules:
  0.0 74.7 jit_solution(13377553977245404892)
XLA Ops:
  0.6 72.2 %shard_map.76 = (f32[4,4,6400]{2,1,0:T(4,128)}, f32[8,128]{1,0:T(8,128)}) custom-call(f32[4,4,6400]{2,1,0:T(4,128)} %psi_in.1, f32[4,6400]{1,0:T(4,128)} %pot_in.1, f32[48,4,6400]{2,1,0:T(4,128)} %bitcast.1, f32[1,2,8]{2,1,0:T(2,128)} %energy_in.1, s32[1,2]{1,0:T(1,128)} %count_in.1), custom_call_target="tpu_custom_call" | custom-call | flops 80000000 | bytes 6000000 | tf_op jit(solution)/shard_map/pallas_call | solution.py:633
  72.8 1.9 %shard_map.77 = (f32[4,4,6400]{2,1,0:T(4,128)}, f32[4,64]{1,0:T(4,128)}, f32[4,64]{1,0:T(4,128)}) custom-call(f32[4,4,6400]{2,1,0:T(4,128)} %get-tuple-element.5.h_in, f32[8,128]{1,0:T(8,128)} %get-tuple-element.6.sums_in), custom_call_target="tpu_custom_call" | custom-call | bytes 900000 | tf_op jit(solution)/shard_map/pallas_call | solution.py:705
